TPU v7x, 32 devices: a whole 2x2x4 slice. The times are simulated.
32 devices in a mesh: walk: 8 (over z, x), pt: 4 (over y, core).
Axes of the slice: x: 2, y: 2, z: 4, core: 2. Of those that a mesh axis runs over, the one named last changes fastest.
Arguments:
- bra_orbitals: bfloat16 [8, 1536, 160], P('walk'), may hold values from -6 to 6
- ket_orbitals: bfloat16 [8, 1536, 160], P('walk'), may hold values from -6 to 6
- collocation: bfloat16 [12288, 1536], P('pt'), may hold values from -0.15625 to 0.15625
- kernel: bfloat16 [12288, 12288], P('pt', 'walk'), as said below
- walker_weight: float32 [8], P('walk'), may hold values from 0.3 to 3
- walker_group: int32 [8], P('walk'), may hold values from 0 to 19
- group_occupied: int32 [20], replicated, may hold values from 80 to 160, as said below
Outputs:
- gradient: float32 [12288, 1536], P('pt', 'walk')
Inputs may be any that keep to these rules, and one draw needn't show every extreme that they name: kernel is symmetric. `group_occupied`: some group has exactly 160 occupied orbitals.
All inputs are finite; a program needn't handle non-finite values.
Results may differ from a plain program's by a relative error of at most 0.0064.
Values may be sent and summed in bfloat16 or wider, within the bound.
No kernel may reach another device: no remote copies, remote signals or barrier semaphores. Data moves between devices by JAX's collectives and lax.ppermute only.
A program may use at most 192 MiB of HBM per device.

v0:
```python
import functools

import jax
import jax.numpy as jnp
from jax import lax
from jax.experimental import pallas as pl
from jax.experimental.pallas import tpu as pltpu
from jax.sharding import PartitionSpec as P

F32 = jnp.float32
BF16 = jnp.bfloat16
BOTH = ("walk", "pt")
NT = (((1,), (1,)), ((), ()))
VMEM_LIMIT = 56 * 1024 * 1024


def tile_of(size, limit):
    return next(t for t in range(min(size, limit), 0, -128) if size % t == 0)


def dot(a, b, dims=(((1,), (0,)), ((), ()))):
    return lax.dot_general(a, b, dims, preferred_element_type=F32)


def cost(flops, nbytes):
    return pl.CostEstimate(flops=flops, bytes_accessed=nbytes, transcendentals=0)


def turn_kernel(in_ref, out_ref):
    out_ref[...] = in_ref[...].T


def turned(block):
    rows, cols = block.shape
    tr, tc = tile_of(rows, 512), tile_of(cols, 512)
    return pl.pallas_call(
        turn_kernel,
        out_shape=jax.ShapeDtypeStruct((cols, rows), block.dtype),
        grid=(cols // tc, rows // tr),
        in_specs=[pl.BlockSpec((tr, tc), lambda c, r: (r, c))],
        out_specs=pl.BlockSpec((tc, tr), lambda c, r: (c, r)),
        compiler_params=pltpu.CompilerParams(vmem_limit_bytes=VMEM_LIMIT),
        cost_estimate=cost(0, 10 * rows * cols),
    )(block)


def pack_kernel(group_ref, occupied_ref, side_ref, weight_ref, bra_ref, ket_ref, own_ref, half_ref):
    occ = bra_ref.shape[0]
    used = occupied_ref[group_ref[0]]
    kept = lax.broadcasted_iota(jnp.int32, bra_ref.shape, 0) < used
    bra_t = jnp.where(kept, bra_ref[...].astype(F32), 0.0).astype(BF16)
    ket_t = jnp.where(kept, ket_ref[...].astype(F32), 0.0).astype(BF16)
    own_ref[:occ, :] = bra_t
    own_ref[occ : 2 * occ, :] = ket_t

    @pl.when(side_ref[0] == 0)
    def _():
        half_ref[:occ, :] = bra_t

    @pl.when(side_ref[0] != 0)
    def _():
        half_ref[:occ, :] = ket_t

    shape = (half_ref.shape[0] - occ, half_ref.shape[1])
    row = lax.broadcasted_iota(jnp.int32, shape, 0)
    rest, rows = jnp.full(shape, weight_ref[0], F32), jnp.zeros(shape, F32)
    for part in range(3):
        near = rest.astype(BF16).astype(F32)
        rows = jnp.where(row == part, near, rows)
        rest = rest - near
    half_ref[occ:, :] = rows.astype(BF16)
    own_ref[2 * occ :, :] = rows.astype(BF16)


def packed(bra, ket, group, occupied, side, weight):
    occ, size_m = bra.shape
    smem = pl.BlockSpec(memory_space=pltpu.SMEM)
    return pl.pallas_call(
        pack_kernel,
        out_shape=[
            jax.ShapeDtypeStruct((2 * occ + 16, size_m), BF16),
            jax.ShapeDtypeStruct((occ + 16, size_m), BF16),
        ],
        in_specs=[smem] * 4 + [pl.BlockSpec(memory_space=pltpu.VMEM)] * 2,
        compiler_params=pltpu.CompilerParams(vmem_limit_bytes=VMEM_LIMIT),
        cost_estimate=cost(0, 12 * size_m * occ),
    )(group, occupied, side, weight, bra, ket)


def project_kernel(rows_each, waits, *refs):
    count = len(rows_each)
    side_ref, items, col_ref = refs[0], refs[1 : count + 1], refs[count + 1]
    out_ref, stack_out, weight_out, stack = refs[count + 2 + waits :]
    occ = min(rows_each)
    width = 2 * occ

    @pl.when(pl.program_id(0) == 0)
    def _():
        at = 0
        weight_out[...] = jnp.zeros_like(weight_out)
        for ref, rows in zip(items, rows_each):
            if rows == occ:
                place = at // width * width + (side_ref[0] if at % width == 0 else 1 - side_ref[0]) * occ
                stack[pl.ds(pl.multiple_of(place, occ), rows), :] = ref[:rows, :]
            else:
                stack[at : at + rows, :] = ref[:rows, :]
            if at % width == 0:
                s = at // width
                weight_out[s : s + 1, :] = jnp.sum(ref[rows : rows + 16, :128].astype(F32), axis=0, keepdims=True)
            at += rows
        stack_out[...] = stack[...]

    out_ref[...] = dot(stack[...], col_ref[...], NT).astype(BF16)


def project(side, items, rows_each, col, groups, index, before=(), after=()):
    size_m, size, total = col.shape[1], col.shape[0], sum(rows_each)
    tile = tile_of(size, 512)
    return pl.pallas_call(
        functools.partial(project_kernel, tuple(rows_each), len(before) + len(after)),
        out_shape=[
            jax.ShapeDtypeStruct((groups * total, size), BF16),
            jax.ShapeDtypeStruct((groups * total, size_m), BF16),
            jax.ShapeDtypeStruct((groups * 8, 128), F32),
        ],
        grid=(size // tile,),
        in_specs=[pl.BlockSpec(memory_space=pltpu.SMEM)]
        + [pl.BlockSpec(x.shape, lambda b: (0, 0), pipeline_mode=pl.Buffered(1)) for x in items]
        + [pl.BlockSpec((tile, size_m), lambda b: (b, 0))]
        + [pl.BlockSpec(memory_space=pl.ANY)] * (len(before) + len(after)),
        out_specs=[
            pl.BlockSpec((total, tile), lambda b: (index, b)),
            pl.BlockSpec((total, size_m), lambda b: (index, 0), pipeline_mode=pl.Buffered(1)),
            pl.BlockSpec((8, 128), lambda b: (index, 0)),
        ],
        scratch_shapes=[pltpu.VMEM((total, size_m), BF16)],
        input_output_aliases={len(items) + 2 + n: n for n in range(len(before))},
        compiler_params=pltpu.CompilerParams(vmem_limit_bytes=VMEM_LIMIT),
        cost_estimate=cost(2 * (total + 640) * size_m * size, 2 * size_m * size),
    )(side, *items, col, *before, *after)


def pair_kernel(sub, weight_ref, block_ref, kt_ref, lrp_ref, lrq_ref, out_ref):
    rows, size_b = kt_ref.shape
    occ = lrp_ref.shape[0] // 4
    sides = [lrq_ref[:, n * occ : (n + 1) * occ] for n in range(4)]
    totals = [jnp.zeros((rows, occ), F32) for _ in range(4)]
    for at in range(0, size_b, sub):
        kern = kt_ref[:, at : at + sub].astype(F32)
        for n in (0, 2):
            left_t = lrp_ref[n * occ : (n + 1) * occ, at : at + sub]
            right_t = lrp_ref[(n + 1) * occ : (n + 2) * occ, at : at + sub]
            had_t = (kern * dot(sides[n + 1], left_t)).astype(BF16)
            had = (kern * dot(sides[n], right_t)).astype(BF16)
            totals[n] += dot(had_t, right_t, NT)
            totals[n + 1] += dot(had, left_t, NT)
    for n in range(4):
        scale = 2.0 * weight_ref[2 * pl.program_id(0) + n // 2]
        out_ref[:, n * occ : (n + 1) * occ] = (totals[n] * scale).astype(BF16)


def pair_gradients(weights, block, kernel_t, lrp, lrq):
    size_b, rows, count = kernel_t.shape[1], lrq.shape[0], weights.shape[0] // 2
    width = lrp.shape[0] // count
    sub = tile_of(size_b, 512)
    return pl.pallas_call(
        functools.partial(pair_kernel, sub),
        out_shape=jax.ShapeDtypeStruct((rows, count * width), BF16),
        grid_spec=pltpu.PrefetchScalarGridSpec(
            num_scalar_prefetch=2,
            grid=(count,),
            in_specs=[
                pl.BlockSpec((rows, size_b), lambda p, w, s: (s[0], 0), pipeline_mode=pl.Buffered(1)),
                pl.BlockSpec((width, size_b), lambda p, w, s: (p, 0)),
                pl.BlockSpec((rows, width), lambda p, w, s: (0, p)),
            ],
            out_specs=pl.BlockSpec((rows, width), lambda p, w, s: (0, p)),
        ),
        compiler_params=pltpu.CompilerParams(vmem_limit_bytes=VMEM_LIMIT),
        cost_estimate=cost(2 * 8 * count * 256 * rows * size_b, 2 * count * (rows + width) * size_b),
    )(weights, block, kernel_t, lrp, lrq)


def send(x, axes, pairs):
    return lax.ppermute(x, axes, pairs)


def masked_orbitals(bra_orbitals, ket_orbitals, walker_group, group_occupied):
    group_count, occ = group_occupied.shape[0], bra_orbitals.shape[2]
    matches = walker_group[:, None] == jnp.arange(group_count, dtype=jnp.int32)[None, :]
    occupied = jnp.sum(jnp.where(matches, group_occupied[None, :], 0), axis=1)
    masks = (jnp.arange(occ, dtype=jnp.int32)[None, :] < occupied[:, None]).astype(BF16)
    bra_t = jnp.swapaxes(bra_orbitals * masks[:, None, :], 1, 2)
    ket_t = jnp.swapaxes(ket_orbitals * masks[:, None, :], 1, 2)
    return jnp.concatenate([bra_t, ket_t], axis=1)


def on_device_8x4(bra, ket, collocation, kernel, walker_weight, walker_group, group_occupied):
    nw, npt = 8, 4
    size_b, size_a = kernel.shape
    occ, size_m = bra.shape
    width = 2 * occ
    me_w, me_p = lax.axis_index("walk"), lax.axis_index("pt")
    z, x, y, core = me_w // 2, me_w % 2, me_p // 2, me_p % 2

    def put(j, i):
        return j * npt + i

    def across(part):
        return send(part, "walk", [(j, j ^ 1) for j in range(nw)])

    def along(part, r):
        return send(part, "walk", [(j, (j - 2 * r) % nw) for j in range(nw)])

    def other(part):
        return send(part, "pt", [(i, i ^ 1) for i in range(npt)])

    tie = lax.optimization_barrier
    half_a = size_a // 2
    rows_alike = lax.dynamic_slice_in_dim(collocation, x * size_a + (1 - core) * half_a, half_a, 0)
    rows_unlike = lax.dynamic_slice_in_dim(collocation, x * size_a + core * half_a, half_a, 0)
    rows_of = [rows_alike]
    for hop, rows in ((1, rows_unlike), (2, rows_alike), (3, rows_unlike)):
        rows_of.append(send(rows, BOTH, [(put(j, j // 2), put(j, j // 2 ^ hop)) for j in range(nw)]))
    own, half = packed(bra, ket, walker_group, group_occupied, core.reshape(1), walker_weight)
    z1, z3, x0 = along(half, 1), along(half, 3), across(half)
    kernel_t = turned(kernel)
    x0, z1, z3, kernel_t = tie((x0, z1, z3, kernel_t))
    z2, x1, x3 = along(z1, 1), across(z1), across(z3)
    z2, z1, z3 = tie((z2, z1, z3))
    token, *rows_of = tie((jnp.zeros((8, 128), F32), *rows_of))
    x2 = across(z2)
    near_four = [own] + [h for part in (x0, z1, z3) for h in (part, other(part))]
    lrp, stack, weight_rows = project(core.reshape(1), near_four, [width] + [occ] * 6, collocation, 2, 0, (), (token,))
    first = (lrp, stack, weight_rows)
    x2, *first = tie((x2, *first))
    far_four = [h for part in (x1, x3, z2, x2) for h in (part, other(part))]
    lrp, stack, weight_rows = project(core.reshape(1), far_four, [occ] * 8, collocation, 2, 1, first)
    weights = jnp.concatenate([weight_rows[:4, 0], weight_rows[8:12, 0]])

    lrq = dot(lax.select_n(me_p ^ z, *rows_of), stack, NT).astype(BF16)
    grads = pair_gradients(weights, (1 - core).reshape(1), kernel_t, lrp, lrq)
    give = dot(grads, stack).astype(BF16)
    give, scale = tie((give, weights))
    grads = pair_gradients(scale, core.reshape(1), kernel_t, lrp, other(lrq))
    part = (dot(grads, stack) + other(give).astype(F32)).reshape(half_a, nw // 2, 2, -1)

    give = lax.dynamic_index_in_dim(part, 1 - y, 2, False).astype(BF16)
    got = send(give, "pt", [(i, i ^ 2) for i in range(npt)])
    part = (lax.dynamic_index_in_dim(part, y, 2, False) + got.astype(F32)).astype(BF16)
    came = []
    for s in range(4):
        pairs = []
        for j in range(nw):
            for i in range(npt):
                pairs.append((put(j, i), put(2 * (s ^ (2 * (j % 2) + i % 2)) + i // 2, j // 2)))
        came.append(send(lax.dynamic_index_in_dim(part, s ^ (2 * x + core), 1, False), BOTH, pairs))
    ordered = [lax.select_n(z, *[came[block ^ s] for s in range(4)]) for block in range(4)]
    return jnp.concatenate(ordered, axis=0).astype(F32) / jnp.sum(weights)


def on_device_any(nw, own, collocation, kernel, walker_weight):
    size_b, size_a = kernel.shape
    size_m = collocation.shape[1]
    me_w, me_p = lax.axis_index("walk"), lax.axis_index("pt")
    weights = lax.all_gather(walker_weight, "walk", axis=0, tiled=True)
    orbitals = lax.all_gather(own, "walk", axis=0, tiled=True)
    all_rows = lax.all_gather(collocation, "pt", axis=0, tiled=True)
    col_q = lax.dynamic_slice_in_dim(all_rows, me_w * size_a, size_a, 0)
    lrp = dot(orbitals, collocation, NT).astype(BF16)
    lrq = dot(col_q, orbitals, NT).astype(BF16)
    grads = pair_gradients(weights / jnp.sum(weights), jnp.zeros(1, jnp.int32), turned(kernel), lrp, lrq)
    part = lax.psum(dot(grads, orbitals), "pt")
    part = jnp.where((me_w * size_a) // size_b == me_p, part, 0.0)
    wide = lax.dynamic_update_slice_in_dim(jnp.zeros((size_b, size_m), F32), part, (me_w * size_a) % size_b, 0)
    return lax.psum_scatter(wide, "walk", scatter_dimension=1, tiled=True)


def on_device(
    nw, npt, bra_orbitals, ket_orbitals, collocation, kernel, walker_weight, walker_group, group_occupied
):
    if (nw, npt, walker_weight.shape[0]) == (8, 4, 1) and kernel.shape[0] == 2 * kernel.shape[1]:
        bra, ket = bra_orbitals[0].T, ket_orbitals[0].T
        return on_device_8x4(bra, ket, collocation, kernel, walker_weight, walker_group, group_occupied)
    own = masked_orbitals(bra_orbitals, ket_orbitals, walker_group, group_occupied)
    return on_device_any(nw, own.reshape(-1, own.shape[2]), collocation, kernel, walker_weight)


def solution(mesh):
    in_specs = (
        P("walk", None, None),
        P("walk", None, None),
        P("pt", None),
        P("pt", "walk"),
        P("walk"),
        P("walk"),
        P(),
    )
    out_specs = P("pt", "walk")
    body = functools.partial(on_device, mesh.shape["walk"], mesh.shape["pt"])
    return jax.shard_map(body, mesh=mesh, in_specs=in_specs, out_specs=out_specs, check_vma=False)
```

profile of v0, /device:TPU:4, one launch (start us, length us, event | category | flops | bytes accessed | tf_op | source)
XLA Modules:
  0.0 322.0 jit_solution(9207720728482769301)
XLA Ops:
  0.0 2.7 constant_dynamic-slice_fusion
  2.7 0.8 collective-permute-start.13
  3.5 1.3 collective-permute-start.14
  4.8 2.1 collective-permute-start.15
  8.2 2.6 shard_map.73
  10.8 1.5 collective-permute-start
  12.3 4.9 %collective-permute-start.1 = (bf16[176,1536]{1,0:T(8,128)(2,1)}, bf16[176,1536]{1,0:T(8,128)(2,1)}, u32[]{:S(2)}, u32[]{:S(2)}) collective-permute-start(bf16[176,1536]{1,0:T(8,128)(2,1)} %get-tuple-element.31), channel_id=1, source_target_pairs={{0,24},{4,28},{8,0},{12,4},{16,8},{20,12},{24,16},{28,20},{1,25},{... | collective-permute-start | bytes 1622024 | tf_op jit(solution)/shard_map/ppermute | solution.py:185
  17.2 7.9 %collective-permute-done.refs_2_ = bf16[176,1536]{1,0:T(8,128)(2,1)} collective-permute-done((bf16[176,1536]{1,0:T(8,128)(2,1)}, bf16[176,1536]{1,0:T(8,128)(2,1)}, u32[]{:S(2)}, u32[]{:S(2)}) %collective-permute-start) | collective-permute-done | bytes 540704 | tf_op jit(solution)/shard_map/ppermute | solution.py:185
  25.1 1.6 collective-permute-start.2
  26.7 14.7 %shard_map.74.kt_ref = bf16[1536,3072]{1,0:T(8,128)(2,1)} custom-call(bf16[3072,1536]{1,0:T(8,128)(2,1)} %in_ref.1), custom_call_target="tpu_custom_call" | custom-call | bytes 47185920 | tf_op jit(solution)/shard_map/pallas_call | solution.py:36
  41.4 0.0 collective-permute-done.1.refs_4_
  41.4 2.1 collective-permute-done.2.refs_6_
  43.5 2.3 collective-permute-start.7
  45.8 0.9 collective-permute-start.3
  46.7 11.3 %collective-permute-done.7.refs_5_ = bf16[176,1536]{1,0:T(8,128)(2,1)S(1)} collective-permute-done((bf16[176,1536]{1,0:T(8,128)(2,1)}, bf16[176,1536]{1,0:T(8,128)(2,1)S(1)}, u32[]{:S(2)}, u32[]{:S(2)}) %collective-permute-start.7) | collective-permute-done | bytes 540704 | tf_op jit(solution)/shard_map/ppermute | solution.py:185
  58.0 0.0 collective-permute-start.10
  58.0 0.0 collective-permute-done.13
  58.0 0.0 copy-start.2
  58.1 1.5 collective-permute-start.5
  59.6 0.0 collective-permute-done.14
  59.6 0.2 collective-permute-start.11
  59.7 0.0 collective-permute-done.15
  59.7 0.4 collective-permute-start.12
  60.1 0.1 collective-permute-done.10.refs_3_
  60.2 1.4 collective-permute-start.9
  61.6 0.0 collective-permute-done.3.refs_1_
  61.6 0.0 collective-permute-start.8
  61.7 11.9 %collective-permute-done.5.refs_3_ = bf16[176,1536]{1,0:T(8,128)(2,1)} collective-permute-done((bf16[176,1536]{1,0:T(8,128)(2,1)}, bf16[176,1536]{1,0:T(8,128)(2,1)}, u32[]{:S(2)}, u32[]{:S(2)}) %collective-permute-start.5) | collective-permute-done | bytes 540704 | tf_op jit(solution)/shard_map/ppermute | solution.py:185
  73.5 0.0 collective-permute-start.4
  73.5 0.0 collective-permute-done.11.refs_5_
  73.5 0.5 collective-permute-start.6
  74.0 0.0 collective-permute-done.12.refs_7_
  74.0 0.6 broadcast_in_dim.3.refs_9_
  74.6 0.2 copy-done.6
  74.8 18.4 %shard_map.75 = (bf16[2560,3072]{1,0:T(8,128)(2,1)}, bf16[2560,1536]{1,0:T(8,128)(2,1)}, f32[16,128]{1,0:T(8,128)}) custom-call(s32[1]{0:T(128)} %bitcast.side_ref.refs_0_.block_ref, bf16[336,1536]{1,0:T(8,128)(2,1)} %get-tuple-element.35.refs_1_, bf16[176,1536]{1,0:T(8,128)(2,1)} %collective-permute-done.refs_2_, bf16[176,1536]{1,0:T(8,128)(2,1)} %copy-done.5, ...), custom_call_target="tpu_custom_call" | custom-call | flops 18119393280 | bytes 9437184 | tf_op jit(solution)/shard_map/pallas_call | solution.py:119
  93.2 0.1 collective-permute-start.16
  93.4 2.2 collective-permute-done.16.refs_8_
  95.6 17.9 %shard_map.76 = (bf16[2560,3072]{1,0:T(8,128)(2,1)}, bf16[2560,1536]{1,0:T(8,128)(2,1)}, f32[16,128]{1,0:T(8,128)}) custom-call(s32[1]{0:T(128)} %bitcast.side_ref.refs_0_.block_ref, bf16[176,1536]{1,0:T(8,128)(2,1)} %copy-done.4, bf16[176,1536]{1,0:T(8,128)(2,1)} %collective-permute-done.4.refs_2_, ...), custom_call_target="tpu_custom_call", output_to_operand_aliasing={{0}: (10, {}), {1}: (11, {}), {2}: (12, {})} | custom-call | flops 18119393280 | bytes 9437184 | tf_op jit(solution)/shard_map/pallas_call | solution.py:119
  113.5 1.4 slice_reduce_fusion
  114.9 10.3 %convolution_convert_fusion.lrq_ref = bf16[768,2560]{1,0:T(8,128)(2,1)S(1)} fusion(bf16[2560,1536]{1,0:T(8,128)(2,1)} %get-tuple-element.54, bf16[768,1536]{1,0:T(8,128)(2,1)} %collective-permute-done.14, bf16[768,1536]{1,0:T(8,128)(2,1)} %collective-permute-done.15, bf16[768,1536]{1,0:T(8,128)(2,1)S(1)} %get-tuple-element.50, ...), kind=kOutput, calls=%fused_computation | convolution fusion | flops 6045302784 | bytes 21233668 | tf_op jit(solution)/shard_map/dot_general | solution.py:22
  125.2 0.2 collective-permute-start.17
  125.4 0.8 pad_maximum_fusion.weight_ref
  126.3 0.9 copy-done
  127.1 46.4 %shard_map.77 = bf16[768,2560]{1,0:T(8,128)(2,1)} custom-call(f32[8]{0:T(128)} %pad_maximum_fusion.weight_ref, s32[1]{0:T(128)} %bitcast.5.block_ref, bf16[1536,3072]{1,0:T(8,128)(2,1)} %shard_map.74.kt_ref, bf16[2560,3072]{1,0:T(8,128)(2,1)} %get-tuple-element.49.lrp_ref, bf16[768,2560]{1,0:T(8,128)(2,1)} %copy-done), custom_call_target="tpu_custom_call" | custom-call | flops 38654705664 | bytes 34603008 | tf_op jit(solution)/shard_map/pallas_call | solution.py:166
  173.6 10.7 %convolution_convert_fusion.1 = bf16[768,1536]{1,0:T(8,128)(2,1)} fusion(bf16[768,2560]{1,0:T(8,128)(2,1)} %shard_map.77, bf16[2560,1536]{1,0:T(8,128)(2,1)} %get-tuple-element.54), kind=kOutput, calls=%fused_computation.2 | convolution fusion | flops 6040977408 | bytes 14155776 | tf_op jit(solution)/shard_map/dot_general | solution.py:22
  184.3 0.1 collective-permute-start.18
  184.5 1.9 copy-done.1
  186.3 46.4 %shard_map.78 = bf16[768,2560]{1,0:T(8,128)(2,1)} custom-call(f32[8]{0:T(128)} %pad_maximum_fusion.weight_ref, s32[1]{0:T(128)} %bitcast.side_ref.refs_0_.block_ref, bf16[1536,3072]{1,0:T(8,128)(2,1)} %shard_map.74.kt_ref, bf16[2560,3072]{1,0:T(8,128)(2,1)} %get-tuple-element.49.lrp_ref, bf16[768,2560]{1,0:T(8,128)(2,1)} %copy-done.1), custom_call_target="tpu_custom_call" | custom-call | flops 38654705664 | bytes 34603008 | tf_op jit(solution)/shard_map/pallas_call | solution.py:166
  232.8 11.6 %convert_add_fusion = f32[768,1536]{1,0:T(8,128)} fusion(bf16[768,1536]{1,0:T(8,128)(2,1)} %collective-permute-done.18, bf16[768,2560]{1,0:T(8,128)(2,1)} %shard_map.78, bf16[2560,1536]{1,0:T(8,128)(2,1)} %get-tuple-element.54), kind=kOutput, calls=%fused_computation.1 | convolution fusion | flops 6042157056 | bytes 18874368 | tf_op jit(solution)/shard_map/dot_general | solution.py:22
  244.3 6.2 %copy.15 = f32[768,1536]{0,1:T(8,128)} copy(f32[768,1536]{1,0:T(8,128)} %convert_add_fusion) | data formatting | bytes 9437184 | tf_op jit(solution)/shard_map/add | solution.py:246
  250.5 1.8 fusion.7
  252.3 0.2 collective-permute-start.19
  252.5 28.1 %collective-permute-done.19 = bf16[768,4,192]{0,2,1:T(8,128)(2,1)S(1)} collective-permute-done((bf16[768,4,192]{0,2,1:T(8,128)(2,1)S(1)}, bf16[768,4,192]{0,2,1:T(8,128)(2,1)S(1)}, u32[]{:S(2)}, u32[]{:S(2)}) %collective-permute-start.19) | collective-permute-done | bytes 1179680 | tf_op jit(solution)/shard_map/ppermute | solution.py:185
  280.6 1.9 fusion
  282.5 0.1 dynamic-slice_bitcast_fusion.1
  282.6 3.1 collective-permute-start.20
  285.7 1.3 collective-permute-start.21
  287.0 4.1 %collective-permute-start.22 = (bf16[768,192]{0,1:T(8,128)(2,1)S(1)}, bf16[768,192]{0,1:T(8,128)(2,1)S(1)}, u32[]{:S(2)}, u32[]{:S(2)}) collective-permute-start(bf16[768,192]{0,1:T(8,128)(2,1)S(1)} %get-tuple-element.67), channel_id=1, source_target_pairs={{0,16},{1,24},{2,20},{3,28},{4,0},{5,8},{6,4},{7,12},{8,17},{9,25}... | collective-permute-start | bytes 884744 | tf_op jit(solution)/shard_map/ppermute | solution.py:185
  291.1 2.1 collective-permute-start.23
  294.6 14.8 %collective-permute-done.20 = bf16[768,192]{0,1:T(8,128)(2,1)S(1)} collective-permute-done((bf16[768,192]{0,1:T(8,128)(2,1)S(1)}, bf16[768,192]{0,1:T(8,128)(2,1)S(1)}, u32[]{:S(2)}, u32[]{:S(2)}) %collective-permute-start.20) | collective-permute-done | bytes 294944 | tf_op jit(solution)/shard_map/ppermute | solution.py:185
  309.4 5.3 %collective-permute-done.21 = bf16[768,192]{0,1:T(8,128)(2,1)S(1)} collective-permute-done((bf16[768,192]{0,1:T(8,128)(2,1)S(1)}, bf16[768,192]{0,1:T(8,128)(2,1)S(1)}, u32[]{:S(2)}, u32[]{:S(2)}) %collective-permute-start.21) | collective-permute-done | bytes 294944 | tf_op jit(solution)/shard_map/ppermute | solution.py:185
  314.7 5.4 %collective-permute-done.23 = bf16[768,192]{0,1:T(8,128)(2,1)S(1)} collective-permute-done((bf16[768,192]{0,1:T(8,128)(2,1)S(1)}, bf16[768,192]{0,1:T(8,128)(2,1)S(1)}, u32[]{:S(2)}, u32[]{:S(2)}) %collective-permute-start.23) | collective-permute-done | bytes 294944 | tf_op jit(solution)/shard_map/ppermute | solution.py:185
  320.1 0.1 select_select_fusion.3
  320.3 1.7 convert_divide_fusion
  (17 shorter events, 0.0 us)
Async XLA Ops:
  2.7 55.4 %collective-permute-start.13 = (bf16[768,1536]{1,0:T(8,128)(2,1)S(1)}, bf16[768,1536]{1,0:T(8,128)(2,1)S(1)}, u32[]{:S(2)}, u32[]{:S(2)}) collective-permute-start(bf16[768,1536]{1,0:T(8,128)(2,1)S(1)} %get-tuple-element.61), channel_id=1, source_target_pairs={{0,1},{4,5},{9,8},{13,12},{18,19},{22,23},{27,26},{31,30}} | collective-permute-start | bytes 7077896 | tf_op jit(solution)/shard_map/ppermute | solution.py:185
  3.5 56.1 %collective-permute-start.14 = (bf16[768,1536]{1,0:T(8,128)(2,1)S(1)}, bf16[768,1536]{1,0:T(8,128)(2,1)}, u32[]{:S(2)}, u32[]{:S(2)}) collective-permute-start(bf16[768,1536]{1,0:T(8,128)(2,1)S(1)} %get-tuple-element.50), channel_id=1, source_target_pairs={{0,2},{4,6},{9,11},{13,15},{18,16},{22,20},{27,25},{31,29}} | collective-permute-start | bytes 7077896 | tf_op jit(solution)/shard_map/ppermute | solution.py:185
  4.8 54.9 %collective-permute-start.15 = (bf16[768,1536]{1,0:T(8,128)(2,1)S(1)}, bf16[768,1536]{1,0:T(8,128)(2,1)}, u32[]{:S(2)}, u32[]{:S(2)}) collective-permute-start(bf16[768,1536]{1,0:T(8,128)(2,1)S(1)} %get-tuple-element.61), channel_id=1, source_target_pairs={{0,3},{4,7},{9,10},{13,14},{18,17},{22,21},{27,24},{31,28}} | collective-permute-start | bytes 7077896 | tf_op jit(solution)/shard_map/ppermute | solution.py:185
  10.8 14.3 %collective-permute-start = (bf16[176,1536]{1,0:T(8,128)(2,1)}, bf16[176,1536]{1,0:T(8,128)(2,1)}, u32[]{:S(2)}, u32[]{:S(2)}) collective-permute-start(bf16[176,1536]{1,0:T(8,128)(2,1)} %get-tuple-element.31), channel_id=1, source_target_pairs={{0,4},{4,0},{8,12},{12,8},{16,20},{20,16},{24,28},{28,24},{1,5},{5... | collective-permute-start | bytes 1622024 | tf_op jit(solution)/shard_map/ppermute | solution.py:185
  12.3 29.1 %collective-permute-start.1 = (bf16[176,1536]{1,0:T(8,128)(2,1)}, bf16[176,1536]{1,0:T(8,128)(2,1)}, u32[]{:S(2)}, u32[]{:S(2)}) collective-permute-start(bf16[176,1536]{1,0:T(8,128)(2,1)} %get-tuple-element.31), channel_id=1, source_target_pairs={{0,24},{4,28},{8,0},{12,4},{16,8},{20,12},{24,16},{28,20},{1,25},{... | collective-permute-start | bytes 1622024 | tf_op jit(solution)/shard_map/ppermute | solution.py:185
  25.1 18.4 %collective-permute-start.2 = (bf16[176,1536]{1,0:T(8,128)(2,1)}, bf16[176,1536]{1,0:T(8,128)(2,1)}, u32[]{:S(2)}, u32[]{:S(2)}) collective-permute-start(bf16[176,1536]{1,0:T(8,128)(2,1)} %get-tuple-element.31), channel_id=1, source_target_pairs={{0,8},{4,12},{8,16},{12,20},{16,24},{20,28},{24,0},{28,4},{1,9},{5... | collective-permute-start | bytes 1622024 | tf_op jit(solution)/shard_map/ppermute | solution.py:185
  43.5 14.5 %collective-permute-start.7 = (bf16[176,1536]{1,0:T(8,128)(2,1)}, bf16[176,1536]{1,0:T(8,128)(2,1)S(1)}, u32[]{:S(2)}, u32[]{:S(2)}) collective-permute-start(bf16[176,1536]{1,0:T(8,128)(2,1)} %collective-permute-done.1.refs_4_), channel_id=1, source_target_pairs={{0,24},{4,28},{8,0},{12,4},{16,8},{20,12},{24,16},{28,20},{1,25},{... | collective-permute-start | bytes 1622024 | tf_op jit(solution)/shard_map/ppermute | solution.py:185
  45.8 15.8 %collective-permute-start.3 = (bf16[176,1536]{1,0:T(8,128)(2,1)}, bf16[176,1536]{1,0:T(8,128)(2,1)S(1)}, u32[]{:S(2)}, u32[]{:S(2)}) collective-permute-start(bf16[176,1536]{1,0:T(8,128)(2,1)} %collective-permute-done.1.refs_4_), channel_id=1, source_target_pairs={{0,4},{4,0},{8,12},{12,8},{16,20},{20,16},{24,28},{28,24},{1,5},{5... | collective-permute-start | bytes 1622024 | tf_op jit(solution)/shard_map/ppermute | solution.py:185
  58.0 35.2 %copy-start.3 = (bf16[176,1536]{1,0:T(8,128)(2,1)}, bf16[176,1536]{1,0:T(8,128)(2,1)S(1)}, u32[]{:S(2)}) copy-start(bf16[176,1536]{1,0:T(8,128)(2,1)S(1)} %collective-permute-done.7.refs_5_) | copy-start | bytes 1622020
  58.0 2.1 collective-permute-start.10
  58.0 35.2 %copy-start.2 = (bf16[768,1536]{1,0:T(8,128)(2,1)}, bf16[768,1536]{1,0:T(8,128)(2,1)S(1)}, u32[]{:S(2)}) copy-start(bf16[768,1536]{1,0:T(8,128)(2,1)S(1)} %collective-permute-done.13) | copy-start | bytes 7077892
  58.1 15.5 %collective-permute-start.5 = (bf16[176,1536]{1,0:T(8,128)(2,1)}, bf16[176,1536]{1,0:T(8,128)(2,1)}, u32[]{:S(2)}, u32[]{:S(2)}) collective-permute-start(bf16[176,1536]{1,0:T(8,128)(2,1)} %collective-permute-done.2.refs_6_), channel_id=1, source_target_pairs={{0,4},{4,0},{8,12},{12,8},{16,20},{20,16},{24,28},{28,24},{1,5},{5... | collective-permute-start | bytes 1622024 | tf_op jit(solution)/shard_map/ppermute | solution.py:185
  59.6 14.0 %collective-permute-start.11 = (bf16[176,1536]{1,0:T(8,128)(2,1)}, bf16[176,1536]{1,0:T(8,128)(2,1)}, u32[]{:S(2)}, u32[]{:S(2)}) collective-permute-start(bf16[176,1536]{1,0:T(8,128)(2,1)} %collective-permute-done.1.refs_4_), channel_id=1, source_target_pairs={{0,1},{1,0},{2,3},{3,2},{4,5},{5,4},{6,7},{7,6},{8,9},{9,8},{10,11... | collective-permute-start | bytes 1622024 | tf_op jit(solution)/shard_map/ppermute | solution.py:185
  59.7 14.3 %collective-permute-start.12 = (bf16[176,1536]{1,0:T(8,128)(2,1)}, bf16[176,1536]{1,0:T(8,128)(2,1)S(1)}, u32[]{:S(2)}, u32[]{:S(2)}) collective-permute-start(bf16[176,1536]{1,0:T(8,128)(2,1)} %collective-permute-done.2.refs_6_), channel_id=1, source_target_pairs={{0,1},{1,0},{2,3},{3,2},{4,5},{5,4},{6,7},{7,6},{8,9},{9,8},{10,11... | collective-permute-start | bytes 1622024 | tf_op jit(solution)/shard_map/ppermute | solution.py:185
  60.2 1.5 copy-start.5
  60.2 33.0 %collective-permute-start.9 = (bf16[176,1536]{1,0:T(8,128)(2,1)S(1)}, bf16[176,1536]{1,0:T(8,128)(2,1)}, u32[]{:S(2)}, u32[]{:S(2)}) collective-permute-start(bf16[176,1536]{1,0:T(8,128)(2,1)S(1)} %collective-permute-done.7.refs_5_), channel_id=1, source_target_pairs={{0,4},{4,0},{8,12},{12,8},{16,20},{20,16},{24,28},{28,24},{1,5},{5... | collective-permute-start | bytes 1622024 | tf_op jit(solution)/shard_map/ppermute | solution.py:185
  61.6 31.6 %copy-start.4 = (bf16[176,1536]{1,0:T(8,128)(2,1)}, bf16[176,1536]{1,0:T(8,128)(2,1)S(1)}, u32[]{:S(2)}) copy-start(bf16[176,1536]{1,0:T(8,128)(2,1)S(1)} %collective-permute-done.3.refs_1_) | copy-start | bytes 1622020
  61.6 31.7 %collective-permute-start.8 = (bf16[176,1536]{1,0:T(8,128)(2,1)S(1)}, bf16[176,1536]{1,0:T(8,128)(2,1)}, u32[]{:S(2)}, u32[]{:S(2)}) collective-permute-start(bf16[176,1536]{1,0:T(8,128)(2,1)S(1)} %collective-permute-done.7.refs_5_), channel_id=1, source_target_pairs={{0,1},{1,0},{2,3},{3,2},{4,5},{5,4},{6,7},{7,6},{8,9},{9,8},{10,11... | collective-permute-start | bytes 1622024 | tf_op jit(solution)/shard_map/ppermute | solution.py:185
  73.5 19.9 %collective-permute-start.4 = (bf16[176,1536]{1,0:T(8,128)(2,1)S(1)}, bf16[176,1536]{1,0:T(8,128)(2,1)}, u32[]{:S(2)}, u32[]{:S(2)}) collective-permute-start(bf16[176,1536]{1,0:T(8,128)(2,1)S(1)} %collective-permute-done.3.refs_1_), channel_id=1, source_target_pairs={{0,1},{1,0},{2,3},{3,2},{4,5},{5,4},{6,7},{7,6},{8,9},{9,8},{10,11... | collective-permute-start | bytes 1622024 | tf_op jit(solution)/shard_map/ppermute | solution.py:185
  73.5 19.9 %collective-permute-start.6 = (bf16[176,1536]{1,0:T(8,128)(2,1)}, bf16[176,1536]{1,0:T(8,128)(2,1)}, u32[]{:S(2)}, u32[]{:S(2)}) collective-permute-start(bf16[176,1536]{1,0:T(8,128)(2,1)} %collective-permute-done.5.refs_3_), channel_id=1, source_target_pairs={{0,1},{1,0},{2,3},{3,2},{4,5},{5,4},{6,7},{7,6},{8,9},{9,8},{10,11... | collective-permute-start | bytes 1622024 | tf_op jit(solution)/shard_map/ppermute | solution.py:185
  74.0 0.8 copy-start.6
  93.2 2.3 collective-permute-start.16
  125.2 1.9 copy-start
  125.2 59.2 %collective-permute-start.17 = (bf16[768,2560]{1,0:T(8,128)(2,1)S(1)}, bf16[768,2560]{1,0:T(8,128)(2,1)S(1)}, u32[]{:S(2)}, u32[]{:S(2)}) collective-permute-start(bf16[768,2560]{1,0:T(8,128)(2,1)S(1)} %convolution_convert_fusion.lrq_ref), channel_id=1, source_target_pairs={{0,1},{1,0},{2,3},{3,2},{4,5},{5,4},{6,7},{7,6},{8,9},{9,8},{10,11... | collective-permute-start | bytes 11796488 | tf_op jit(solution)/shard_map/ppermute | solution.py:185
  184.3 48.4 %collective-permute-start.18 = (bf16[768,1536]{1,0:T(8,128)(2,1)}, bf16[768,1536]{1,0:T(8,128)(2,1)}, u32[]{:S(2)}, u32[]{:S(2)}) collective-permute-start(bf16[768,1536]{1,0:T(8,128)(2,1)} %convolution_convert_fusion.1), channel_id=1, source_target_pairs={{0,1},{1,0},{2,3},{3,2},{4,5},{5,4},{6,7},{7,6},{8,9},{9,8},{10,11... | collective-permute-start | bytes 7077896 | tf_op jit(solution)/shard_map/ppermute | solution.py:185
  184.5 1.9 copy-start.1
  252.3 28.3 %collective-permute-start.19 = (bf16[768,4,192]{0,2,1:T(8,128)(2,1)S(1)}, bf16[768,4,192]{0,2,1:T(8,128)(2,1)S(1)}, u32[]{:S(2)}, u32[]{:S(2)}) collective-permute-start(bf16[768,4,192]{0,2,1:T(8,128)(2,1)S(1)} %fusion.7), channel_id=1, source_target_pairs={{0,2},{1,3},{2,0},{3,1},{4,6},{5,7},{6,4},{7,5},{8,10},{9,11},{10,... | collective-permute-start | bytes 3538952 | tf_op jit(solution)/shard_map/ppermute | solution.py:185
  282.6 26.8 %collective-permute-start.20 = (bf16[768,192]{0,1:T(8,128)(2,1)S(1)}, bf16[768,192]{0,1:T(8,128)(2,1)S(1)}, u32[]{:S(2)}, u32[]{:S(2)}) collective-permute-start(bf16[768,192]{0,1:T(8,128)(2,1)S(1)} %get-tuple-element.70), channel_id=1, source_target_pairs={{0,0},{1,8},{2,4},{3,12},{4,16},{5,24},{6,20},{7,28},{8,1},{9,9},{... | collective-permute-start | bytes 884744 | tf_op jit(solution)/shard_map/ppermute | solution.py:185
  285.7 29.0 %collective-permute-start.21 = (bf16[768,192]{0,1:T(8,128)(2,1)S(1)}, bf16[768,192]{0,1:T(8,128)(2,1)S(1)}, u32[]{:S(2)}, u32[]{:S(2)}) collective-permute-start(bf16[768,192]{0,1:T(8,128)(2,1)S(1)} %get-tuple-element.69), channel_id=1, source_target_pairs={{0,8},{1,0},{2,12},{3,4},{4,24},{5,16},{6,28},{7,20},{8,9},{9,1},{... | collective-permute-start | bytes 884744 | tf_op jit(solution)/shard_map/ppermute | solution.py:185
  287.0 27.7 %collective-permute-start.22 = (bf16[768,192]{0,1:T(8,128)(2,1)S(1)}, bf16[768,192]{0,1:T(8,128)(2,1)S(1)}, u32[]{:S(2)}, u32[]{:S(2)}) collective-permute-start(bf16[768,192]{0,1:T(8,128)(2,1)S(1)} %get-tuple-element.67), channel_id=1, source_target_pairs={{0,16},{1,24},{2,20},{3,28},{4,0},{5,8},{6,4},{7,12},{8,17},{9,25}... | collective-permute-start | bytes 884744 | tf_op jit(solution)/shard_map/ppermute | solution.py:185
  291.1 29.0 %collective-permute-start.23 = (bf16[768,192]{0,1:T(8,128)(2,1)S(1)}, bf16[768,192]{0,1:T(8,128)(2,1)S(1)}, u32[]{:S(2)}, u32[]{:S(2)}) collective-permute-start(bf16[768,192]{0,1:T(8,128)(2,1)S(1)} %get-tuple-element.68), channel_id=1, source_target_pairs={{0,24},{1,16},{2,28},{3,20},{4,8},{5,0},{6,12},{7,4},{8,25},{9,17}... | collective-permute-start | bytes 884744 | tf_op jit(solution)/shard_map/ppermute | solution.py:185
where the time goes:
time: 323 us; the launch traced here: 322 us
  Pallas kernels  146 us (45%)
  waiting for transfers between devices  89.2 us (28%)
  matrix products  32.7 us (10%)
  starting transfers between devices  30.7 us (10%)
  local copies, waits for them, and re-layouts  14.3 us (4%)
  other arithmetic  5.95 us (2%)
    pallas_call x2, Pallas kernels, pair_gradients(): pl.pallas_call(functools.partial(pair_kernel, sub), out_shape=jax.ShapeDt...  92.8 us
    ppermute x24, waiting for transfers between devices, send(): return lax.ppermute(x, axes, pairs)  89.2 us
    pallas_call x2, Pallas kernels, project(): pl.pallas_call(functools.partial(project_kernel, tuple(rows_each), len(be...  36.3 us
    dot_general x3, matrix products, dot(): return lax.dot_general(a, b, dims, preferred_element_type=F32)  32.7 us
    ppermute x24, starting transfers between devices, send(): return lax.ppermute(x, axes, pairs)  30.7 us
    pallas_call x1, Pallas kernels, turned(): pl.pallas_call(turn_kernel, out_shape=jax.ShapeDtypeStruct((cols, rows),...  14.7 us
  transfers between devices with their start and end apart: 24, of which 10 were waited for; matrix products, arithmetic and copies ran while one was open for 4% of the time, Pallas kernels for 40%

commit v1 on v0

--- a/solution.py
+++ b/solution.py
@@ -113,11 +113,11 @@
     out_ref[...] = dot(stack[...], col_ref[...], NT).astype(BF16)
 
 
-def project(side, items, rows_each, col, groups, index, before=(), after=()):
+def project(side, items, rows_each, col, groups, index, before=()):
     size_m, size, total = col.shape[1], col.shape[0], sum(rows_each)
     tile = tile_of(size, 512)
     return pl.pallas_call(
-        functools.partial(project_kernel, tuple(rows_each), len(before) + len(after)),
+        functools.partial(project_kernel, tuple(rows_each), len(before)),
         out_shape=[
             jax.ShapeDtypeStruct((groups * total, size), BF16),
             jax.ShapeDtypeStruct((groups * total, size_m), BF16),
@@ -127,7 +127,7 @@
         in_specs=[pl.BlockSpec(memory_space=pltpu.SMEM)]
         + [pl.BlockSpec(x.shape, lambda b: (0, 0), pipeline_mode=pl.Buffered(1)) for x in items]
         + [pl.BlockSpec((tile, size_m), lambda b: (b, 0))]
-        + [pl.BlockSpec(memory_space=pl.ANY)] * (len(before) + len(after)),
+        + [pl.BlockSpec(memory_space=pl.ANY)] * (len(before)),
         out_specs=[
             pl.BlockSpec((total, tile), lambda b: (index, b)),
             pl.BlockSpec((total, size_m), lambda b: (index, 0), pipeline_mode=pl.Buffered(1)),
@@ -137,7 +137,7 @@
         input_output_aliases={len(items) + 2 + n: n for n in range(len(before))},
         compiler_params=pltpu.CompilerParams(vmem_limit_bytes=VMEM_LIMIT),
         cost_estimate=cost(2 * (total + 640) * size_m * size, 2 * size_m * size),
-    )(side, *items, col, *before, *after)
+    )(side, *items, col, *before)
 
 
 def pair_kernel(sub, weight_ref, block_ref, kt_ref, lrp_ref, lrq_ref, out_ref):
@@ -219,44 +219,47 @@
     half_a = size_a // 2
     rows_alike = lax.dynamic_slice_in_dim(collocation, x * size_a + (1 - core) * half_a, half_a, 0)
     rows_unlike = lax.dynamic_slice_in_dim(collocation, x * size_a + core * half_a, half_a, 0)
-    rows_of = [rows_alike]
-    for hop, rows in ((1, rows_unlike), (2, rows_alike), (3, rows_unlike)):
-        rows_of.append(send(rows, BOTH, [(put(j, j // 2), put(j, j // 2 ^ hop)) for j in range(nw)]))
+    over = [(put(j, j // 2), put(j, j // 2 ^ 2)) for j in range(nw)]
+    far_alike, far_unlike = send(rows_alike, BOTH, over), send(rows_unlike, BOTH, over)
     own, half = packed(bra, ket, walker_group, group_occupied, core.reshape(1), walker_weight)
     z1, z3, x0 = along(half, 1), along(half, 3), across(half)
     kernel_t = turned(kernel)
     x0, z1, z3, kernel_t = tie((x0, z1, z3, kernel_t))
     z2, x1, x3 = along(z1, 1), across(z1), across(z3)
     z2, z1, z3 = tie((z2, z1, z3))
-    token, *rows_of = tie((jnp.zeros((8, 128), F32), *rows_of))
     x2 = across(z2)
     near_four = [own] + [h for part in (x0, z1, z3) for h in (part, other(part))]
-    lrp, stack, weight_rows = project(core.reshape(1), near_four, [width] + [occ] * 6, collocation, 2, 0, (), (token,))
+    lrp, stack, weight_rows = project(core.reshape(1), near_four, [width] + [occ] * 6, collocation, 2, 0)
+    far_alike, far_unlike, weight_rows = tie((far_alike, far_unlike, weight_rows))
     first = (lrp, stack, weight_rows)
     x2, *first = tie((x2, *first))
     far_four = [h for part in (x1, x3, z2, x2) for h in (part, other(part))]
     lrp, stack, weight_rows = project(core.reshape(1), far_four, [occ] * 8, collocation, 2, 1, first)
     weights = jnp.concatenate([weight_rows[:4, 0], weight_rows[8:12, 0]])
 
-    lrq = dot(lax.select_n(me_p ^ z, *rows_of), stack, NT).astype(BF16)
+    beside = [(put(j, j // 2 ^ s), put(j, j // 2 ^ s ^ 1)) for j in range(nw) for s in (0, 2)]
+    beside = send(jnp.where(me_p == z, rows_unlike, far_unlike), BOTH, beside)
+    col_q = jnp.where(core != z % 2, beside, jnp.where(me_p == z, rows_alike, far_alike))
+    lrq = dot(col_q, stack, NT).astype(BF16)
     grads = pair_gradients(weights, (1 - core).reshape(1), kernel_t, lrp, lrq)
-    give = dot(grads, stack).astype(BF16)
+    by_rows = (((0,), (1,)), ((), ()))
+    give = dot(stack, grads, by_rows).astype(BF16)
     give, scale = tie((give, weights))
     grads = pair_gradients(scale, core.reshape(1), kernel_t, lrp, other(lrq))
-    part = (dot(grads, stack) + other(give).astype(F32)).reshape(half_a, nw // 2, 2, -1)
-
-    give = lax.dynamic_index_in_dim(part, 1 - y, 2, False).astype(BF16)
+    part = (dot(stack, grads, by_rows) + other(give).astype(F32)).reshape(nw // 2, 2, -1, half_a)
+
+    give = lax.dynamic_index_in_dim(part, 1 - y, 1, False).astype(BF16)
     got = send(give, "pt", [(i, i ^ 2) for i in range(npt)])
-    part = (lax.dynamic_index_in_dim(part, y, 2, False) + got.astype(F32)).astype(BF16)
+    part = (lax.dynamic_index_in_dim(part, y, 1, False) + got.astype(F32)).astype(BF16)
     came = []
     for s in range(4):
         pairs = []
         for j in range(nw):
             for i in range(npt):
                 pairs.append((put(j, i), put(2 * (s ^ (2 * (j % 2) + i % 2)) + i // 2, j // 2)))
-        came.append(send(lax.dynamic_index_in_dim(part, s ^ (2 * x + core), 1, False), BOTH, pairs))
+        came.append(send(lax.dynamic_index_in_dim(part, s ^ (2 * x + core), 0, False), BOTH, pairs))
     ordered = [lax.select_n(z, *[came[block ^ s] for s in range(4)]) for block in range(4)]
-    return jnp.concatenate(ordered, axis=0).astype(F32) / jnp.sum(weights)
+    return (jnp.concatenate(ordered, axis=1).astype(F32) / jnp.sum(weights)).T
 
 
 def on_device_any(nw, own, collocation, kernel, walker_weight):

time: 323 us -> 319 us (0.988)
  the two profiles are of different devices: /device:TPU:4 before, /device:TPU:19 now
where the time goes in v1:
time: 319 us; the launch traced here: 318 us
  Pallas kernels  146 us (46%)
  waiting for transfers between devices  80.9 us (25%)
  starting transfers between devices  38.5 us (12%)
  matrix products  31 us (10%)
  local copies, waits for them, and re-layouts  9.6 us (3%)
  other arithmetic  9.12 us (3%)
    pallas_call x2, Pallas kernels, pair_gradients(): pl.pallas_call(functools.partial(pair_kernel, sub), out_shape=jax.ShapeDt...  92.8 us
    ppermute x24, waiting for transfers between devices, send(): return lax.ppermute(x, axes, pairs)  80.9 us
    ppermute x24, starting transfers between devices, send(): return lax.ppermute(x, axes, pairs)  38.5 us
    pallas_call x2, Pallas kernels, project(): pl.pallas_call(functools.partial(project_kernel, tuple(rows_each), len(be...  36.4 us
    dot_general x3, matrix products, dot(): return lax.dot_general(a, b, dims, preferred_element_type=F32)  31 us
    pallas_call x1, Pallas kernels, turned(): pl.pallas_call(turn_kernel, out_shape=jax.ShapeDtypeStruct((cols, rows),...  14.7 us
  transfers between devices with their start and end apart: 24, of which 9 were waited for; matrix products, arithmetic and copies ran while one was open for 6% of the time, Pallas kernels for 45%

profile of v1, /device:TPU:19, one launch (start us, length us, event | category | flops | bytes accessed | tf_op | source)
XLA Modules:
  0.0 318.5 jit_solution(12452847705451093915)
XLA Ops:
  1.3 2.6 shard_map.73
  3.9 1.3 collective-permute-start.2
  5.2 0.2 collective-permute-start.1
  5.3 0.3 collective-permute-start
  5.6 14.7 %shard_map.74.kt_ref = bf16[1536,3072]{1,0:T(8,128)(2,1)} custom-call(bf16[3072,1536]{1,0:T(8,128)(2,1)} %in_ref.1), custom_call_target="tpu_custom_call" | custom-call | bytes 47185920 | tf_op jit(solution)/shard_map/pallas_call | solution.py:36
  20.3 8.6 %collective-permute-done.1.refs_4_ = bf16[176,1536]{1,0:T(8,128)(2,1)S(1)} collective-permute-done((bf16[176,1536]{1,0:T(8,128)(2,1)}, bf16[176,1536]{1,0:T(8,128)(2,1)S(1)}, u32[]{:S(2)}, u32[]{:S(2)}) %collective-permute-start.1) | collective-permute-done | bytes 540704 | tf_op jit(solution)/shard_map/ppermute | solution.py:185
  28.9 0.0 collective-permute-done.refs_2_
  28.9 2.0 collective-permute-start.7
  30.9 4.1 %constant_dynamic-slice_fusion = (bf16[768,1536]{1,0:T(8,128)(2,1)S(1)}, bf16[768,1536]{1,0:T(8,128)(2,1)}) fusion(bf16[3072,1536]{1,0:T(8,128)(2,1)} %refs_9_.1, s32[]{:T(128)S(6)} %select_n.146, s32[]{:T(128)S(6)} %select_n.145), kind=kLoop, calls=%fused_computation.21 | loop fusion | bytes 9437192 | tf_op jit(solution)/shard_map/dynamic_slice | solution.py:221
  35.0 2.1 collective-permute-start.14
  37.1 2.1 collective-permute-start.13
  39.1 0.0 collective-permute-start.10
  39.2 2.9 collective-permute-done.7.refs_5_
  42.0 1.5 collective-permute-start.11
  43.6 0.0 collective-permute-start.12
  43.6 0.0 collective-permute-done.10.refs_3_
  43.6 0.5 collective-permute-start.5
  44.1 1.9 collective-permute-done.11.refs_5_
  46.0 0.5 collective-permute-start.3
  46.5 1.0 collective-permute-start.9
  47.5 18.5 %shard_map.75 = (bf16[2560,3072]{1,0:T(8,128)(2,1)}, bf16[2560,1536]{1,0:T(8,128)(2,1)}, f32[16,128]{1,0:T(8,128)}) custom-call(s32[1]{0:T(128)} %bitcast.side_ref.refs_0_.block_ref, bf16[336,1536]{1,0:T(8,128)(2,1)} %get-tuple-element.33.refs_1_, bf16[176,1536]{1,0:T(8,128)(2,1)} %collective-permute-done.refs_2_, ...), custom_call_target="tpu_custom_call" | custom-call | flops 18119393280 | bytes 9437184 | tf_op jit(solution)/shard_map/pallas_call | solution.py:119
  66.0 1.0 collective-permute-start.8
  67.0 1.8 collective-permute-done.3.refs_1_
  68.8 2.3 collective-permute-start.6
  71.1 0.0 collective-permute-done.14
  71.1 0.0 collective-permute-start.4
  71.1 9.3 %collective-permute-done.9.refs_7_ = bf16[176,1536]{1,0:T(8,128)(2,1)} collective-permute-done((bf16[176,1536]{1,0:T(8,128)(2,1)S(1)}, bf16[176,1536]{1,0:T(8,128)(2,1)}, u32[]{:S(2)}, u32[]{:S(2)}) %collective-permute-start.9) | collective-permute-done | bytes 540704 | tf_op jit(solution)/shard_map/ppermute | solution.py:185
  80.4 11.5 %collective-permute-start.15 = (bf16[176,1536]{1,0:T(8,128)(2,1)}, bf16[176,1536]{1,0:T(8,128)(2,1)}, u32[]{:S(2)}, u32[]{:S(2)}) collective-permute-start(bf16[176,1536]{1,0:T(8,128)(2,1)} %collective-permute-done.9.refs_7_), channel_id=1, source_target_pairs={{0,1},{1,0},{2,3},{3,2},{4,5},{5,4},{6,7},{7,6},{8,9},{9,8},{10,11... | collective-permute-start | bytes 1622024 | tf_op jit(solution)/shard_map/ppermute | solution.py:185
  91.9 3.3 %broadcast_select_fusion = bf16[768,1536]{1,0:T(8,128)(2,1)} fusion(bf16[768,1536]{1,0:T(8,128)(2,1)S(1)} %get-tuple-element.57, bf16[768,1536]{1,0:T(8,128)(2,1)} %collective-permute-done.14, pred[]{:T(512)S(6)} %eq.8), kind=kLoop, calls=%fused_computation.10 | loop fusion | flops 1179648 | bytes 7077889 | tf_op jit(solution)/shard_map/jit(_where)/select_n | solution.py:241
  95.2 1.3 collective-permute-start.16
  96.5 0.0 collective-permute-done.6.refs_4_
  96.6 0.0 collective-permute-done.8.refs_6_
  96.6 0.0 collective-permute-done.15.refs_8_
  96.6 0.8 copy-done.5
  97.3 17.9 %shard_map.76 = (bf16[2560,3072]{1,0:T(8,128)(2,1)}, bf16[2560,1536]{1,0:T(8,128)(2,1)}, f32[16,128]{1,0:T(8,128)}) custom-call(s32[1]{0:T(128)} %bitcast.side_ref.refs_0_.block_ref, bf16[176,1536]{1,0:T(8,128)(2,1)} %collective-permute-done.3.refs_1_, ...), custom_call_target="tpu_custom_call", output_to_operand_aliasing={{0}: (10, {}), {1}: (11, {}), {2}: (12, {})} | custom-call | flops 18119393280 | bytes 9437184 | tf_op jit(solution)/shard_map/pallas_call | solution.py:119
  115.2 1.4 slice_reduce_fusion
  116.6 0.7 pad_maximum_fusion.weight_ref
  117.3 0.0 collective-permute-done.16
  117.3 9.6 %convolution_convert_fusion.lrq_ref = bf16[768,2560]{1,0:T(8,128)(2,1)S(1)} fusion(bf16[2560,1536]{1,0:T(8,128)(2,1)} %get-tuple-element.45, bf16[768,1536]{1,0:T(8,128)(2,1)S(1)} %collective-permute-done.16, bf16[768,1536]{1,0:T(8,128)(2,1)} %get-tuple-element.58, bf16[768,1536]{1,0:T(8,128)(2,1)} %collective-permute-done.13, pred[]{:T(512)S(6)} %eq.8, ...), kind=kOutput, calls=%fused_computation | convolution fusion | flops 6044123136 | bytes 18874370 | tf_op jit(solution)/shard_map/dot_general | solution.py:22
  126.9 1.3 collective-permute-start.17
  128.2 0.5 copy-done.1
  128.8 46.4 %shard_map.77 = bf16[768,2560]{1,0:T(8,128)(2,1)} custom-call(f32[8]{0:T(128)} %pad_maximum_fusion.weight_ref, s32[1]{0:T(128)} %bitcast.5.block_ref, bf16[1536,3072]{1,0:T(8,128)(2,1)} %shard_map.74.kt_ref, bf16[2560,3072]{1,0:T(8,128)(2,1)} %get-tuple-element.48.lrp_ref, bf16[768,2560]{1,0:T(8,128)(2,1)} %copy-done.1), custom_call_target="tpu_custom_call" | custom-call | flops 38654705664 | bytes 34603008 | tf_op jit(solution)/shard_map/pallas_call | solution.py:166
  175.2 10.9 %convolution_convert_fusion.1 = bf16[1536,768]{1,0:T(8,128)(2,1)} fusion(bf16[2560,1536]{1,0:T(8,128)(2,1)} %get-tuple-element.45, bf16[768,2560]{1,0:T(8,128)(2,1)} %shard_map.77), kind=kOutput, calls=%fused_computation.2 | convolution fusion | flops 6040977408 | bytes 14155776 | tf_op jit(solution)/shard_map/dot_general | solution.py:22
  186.1 1.3 collective-permute-start.18
  187.3 0.0 collective-permute-done.17.lrq_ref
  187.3 1.9 copy-done.2
  189.2 46.4 %shard_map.78 = bf16[768,2560]{1,0:T(8,128)(2,1)} custom-call(f32[8]{0:T(128)} %pad_maximum_fusion.weight_ref, s32[1]{0:T(128)} %bitcast.side_ref.refs_0_.block_ref, bf16[1536,3072]{1,0:T(8,128)(2,1)} %shard_map.74.kt_ref, bf16[2560,3072]{1,0:T(8,128)(2,1)} %get-tuple-element.48.lrp_ref, bf16[768,2560]{1,0:T(8,128)(2,1)} %copy-done.2), custom_call_target="tpu_custom_call" | custom-call | flops 38654705664 | bytes 34603008 | tf_op jit(solution)/shard_map/pallas_call | solution.py:166
  235.6 0.0 collective-permute-done.18
  235.6 10.5 %convert_add_fusion = f32[1536,768]{1,0:T(8,128)S(1)} fusion(bf16[1536,768]{1,0:T(8,128)(2,1)} %collective-permute-done.18, bf16[2560,1536]{1,0:T(8,128)(2,1)} %get-tuple-element.45, bf16[768,2560]{1,0:T(8,128)(2,1)} %shard_map.78), kind=kOutput, calls=%fused_computation.1 | convolution fusion | flops 6042157056 | bytes 18874368 | tf_op jit(solution)/shard_map/dot_general | solution.py:22
  246.1 2.1 copy-done
  248.2 0.1 fusion.5
  248.4 0.1 collective-permute-start.19
  248.5 27.6 %collective-permute-done.19 = bf16[4,192,768]{2,1,0:T(8,128)(2,1)S(1)} collective-permute-done((bf16[4,192,768]{2,1,0:T(8,128)(2,1)S(1)}, bf16[4,192,768]{2,1,0:T(8,128)(2,1)S(1)}, u32[]{:S(2)}, u32[]{:S(2)}) %collective-permute-start.19) | collective-permute-done | bytes 1179680 | tf_op jit(solution)/shard_map/ppermute | solution.py:185
  276.0 1.9 fusion
  277.9 0.1 dynamic-slice_bitcast_fusion.1
  278.0 0.1 collective-permute-start.22
  278.1 5.1 %collective-permute-start.23 = (bf16[192,768]{1,0:T(8,128)(2,1)S(1)}, bf16[192,768]{1,0:T(8,128)(2,1)S(1)}, u32[]{:S(2)}, u32[]{:S(2)}) collective-permute-start(bf16[192,768]{1,0:T(8,128)(2,1)S(1)} %get-tuple-element.64), channel_id=1, source_target_pairs={{0,24},{1,16},{2,28},{3,20},{4,8},{5,0},{6,12},{7,4},{8,25},{9,17}... | collective-permute-start | bytes 884744 | tf_op jit(solution)/shard_map/ppermute | solution.py:185
  283.2 1.3 collective-permute-start.21
  284.5 1.9 collective-permute-start.20
  287.8 18.4 %collective-permute-done.22 = bf16[192,768]{1,0:T(8,128)(2,1)S(1)} collective-permute-done((bf16[192,768]{1,0:T(8,128)(2,1)S(1)}, bf16[192,768]{1,0:T(8,128)(2,1)S(1)}, u32[]{:S(2)}, u32[]{:S(2)}) %collective-permute-start.22) | collective-permute-done | bytes 294944 | tf_op jit(solution)/shard_map/ppermute | solution.py:185
  306.2 4.3 %collective-permute-done.21 = bf16[192,768]{1,0:T(8,128)(2,1)S(1)} collective-permute-done((bf16[192,768]{1,0:T(8,128)(2,1)S(1)}, bf16[192,768]{1,0:T(8,128)(2,1)S(1)}, u32[]{:S(2)}, u32[]{:S(2)}) %collective-permute-start.21) | collective-permute-done | bytes 294944 | tf_op jit(solution)/shard_map/ppermute | solution.py:185
  310.5 6.1 %collective-permute-done.20 = bf16[192,768]{1,0:T(8,128)(2,1)S(1)} collective-permute-done((bf16[192,768]{1,0:T(8,128)(2,1)S(1)}, bf16[192,768]{1,0:T(8,128)(2,1)S(1)}, u32[]{:S(2)}, u32[]{:S(2)}) %collective-permute-start.20) | collective-permute-done | bytes 294944 | tf_op jit(solution)/shard_map/ppermute | solution.py:185
  316.6 0.1 select_select_fusion.3
  316.8 1.7 divide_bitcast_fusion
  (14 shorter events, 0.0 us)
Async XLA Ops:
  3.9 16.4 %collective-permute-start.2 = (bf16[176,1536]{1,0:T(8,128)(2,1)}, bf16[176,1536]{1,0:T(8,128)(2,1)}, u32[]{:S(2)}, u32[]{:S(2)}) collective-permute-start(bf16[176,1536]{1,0:T(8,128)(2,1)} %get-tuple-element.29), channel_id=1, source_target_pairs={{0,8},{4,12},{8,16},{12,20},{16,24},{20,28},{24,0},{28,4},{1,9},{5... | collective-permute-start | bytes 1622024 | tf_op jit(solution)/shard_map/ppermute | solution.py:185
  5.2 23.7 %collective-permute-start.1 = (bf16[176,1536]{1,0:T(8,128)(2,1)}, bf16[176,1536]{1,0:T(8,128)(2,1)S(1)}, u32[]{:S(2)}, u32[]{:S(2)}) collective-permute-start(bf16[176,1536]{1,0:T(8,128)(2,1)} %get-tuple-element.29), channel_id=1, source_target_pairs={{0,24},{4,28},{8,0},{12,4},{16,8},{20,12},{24,16},{28,20},{1,25},{... | collective-permute-start | bytes 1622024 | tf_op jit(solution)/shard_map/ppermute | solution.py:185
  5.3 23.5 %collective-permute-start = (bf16[176,1536]{1,0:T(8,128)(2,1)}, bf16[176,1536]{1,0:T(8,128)(2,1)}, u32[]{:S(2)}, u32[]{:S(2)}) collective-permute-start(bf16[176,1536]{1,0:T(8,128)(2,1)} %get-tuple-element.29), channel_id=1, source_target_pairs={{0,4},{4,0},{8,12},{12,8},{16,20},{20,16},{24,28},{28,24},{1,5},{5... | collective-permute-start | bytes 1622024 | tf_op jit(solution)/shard_map/ppermute | solution.py:185
  28.9 17.1 %copy-start.4 = (bf16[176,1536]{1,0:T(8,128)(2,1)}, bf16[176,1536]{1,0:T(8,128)(2,1)S(1)}, u32[]{:S(2)}) copy-start(bf16[176,1536]{1,0:T(8,128)(2,1)S(1)} %collective-permute-done.1.refs_4_) | copy-start | bytes 1622020
  28.9 13.2 %collective-permute-start.7 = (bf16[176,1536]{1,0:T(8,128)(2,1)S(1)}, bf16[176,1536]{1,0:T(8,128)(2,1)S(1)}, u32[]{:S(2)}, u32[]{:S(2)}) collective-permute-start(bf16[176,1536]{1,0:T(8,128)(2,1)S(1)} %collective-permute-done.1.refs_4_), channel_id=1, source_target_pairs={{0,24},{4,28},{8,0},{12,4},{16,8},{20,12},{24,16},{28,20},{1,25},{... | collective-permute-start | bytes 1622024 | tf_op jit(solution)/shard_map/ppermute | solution.py:185
  35.0 36.2 %collective-permute-start.14 = (bf16[768,1536]{1,0:T(8,128)(2,1)S(1)}, bf16[768,1536]{1,0:T(8,128)(2,1)}, u32[]{:S(2)}, u32[]{:S(2)}) collective-permute-start(bf16[768,1536]{1,0:T(8,128)(2,1)S(1)} %get-tuple-element.57), channel_id=1, source_target_pairs={{0,2},{4,6},{9,11},{13,15},{18,16},{22,20},{27,25},{31,29}} | collective-permute-start | bytes 7077896 | tf_op jit(solution)/shard_map/ppermute | solution.py:185
  37.1 34.1 %collective-permute-start.13 = (bf16[768,1536]{1,0:T(8,128)(2,1)}, bf16[768,1536]{1,0:T(8,128)(2,1)}, u32[]{:S(2)}, u32[]{:S(2)}) collective-permute-start(bf16[768,1536]{1,0:T(8,128)(2,1)} %get-tuple-element.58), channel_id=1, source_target_pairs={{0,2},{4,6},{9,11},{13,15},{18,16},{22,20},{27,25},{31,29}} | collective-permute-start | bytes 7077896 | tf_op jit(solution)/shard_map/ppermute | solution.py:185
  39.1 4.4 %collective-permute-start.10 = (bf16[176,1536]{1,0:T(8,128)(2,1)}, bf16[176,1536]{1,0:T(8,128)(2,1)}, u32[]{:S(2)}, u32[]{:S(2)}) collective-permute-start(bf16[176,1536]{1,0:T(8,128)(2,1)} %collective-permute-done.refs_2_), channel_id=1, source_target_pairs={{0,1},{1,0},{2,3},{3,2},{4,5},{5,4},{6,7},{7,6},{8,9},{9,8},{10,11... | collective-permute-start | bytes 1622024 | tf_op jit(solution)/shard_map/ppermute | solution.py:185
  42.0 24.0 %copy-start.3 = (bf16[176,1536]{1,0:T(8,128)(2,1)}, bf16[176,1536]{1,0:T(8,128)(2,1)S(1)}, u32[]{:S(2)}) copy-start(bf16[176,1536]{1,0:T(8,128)(2,1)S(1)} %collective-permute-done.7.refs_5_) | copy-start | bytes 1622020
  42.0 4.0 %collective-permute-start.11 = (bf16[176,1536]{1,0:T(8,128)(2,1)S(1)}, bf16[176,1536]{1,0:T(8,128)(2,1)}, u32[]{:S(2)}, u32[]{:S(2)}) collective-permute-start(bf16[176,1536]{1,0:T(8,128)(2,1)S(1)} %collective-permute-done.1.refs_4_), channel_id=1, source_target_pairs={{0,1},{1,0},{2,3},{3,2},{4,5},{5,4},{6,7},{7,6},{8,9},{9,8},{10,11... | collective-permute-start | bytes 1622024 | tf_op jit(solution)/shard_map/ppermute | solution.py:185
  43.6 2.9 collective-permute-start.12
  43.6 22.4 %collective-permute-start.5 = (bf16[176,1536]{1,0:T(8,128)(2,1)}, bf16[176,1536]{1,0:T(8,128)(2,1)}, u32[]{:S(2)}, u32[]{:S(2)}) collective-permute-start(bf16[176,1536]{1,0:T(8,128)(2,1)} %collective-permute-done.2.refs_6_), channel_id=1, source_target_pairs={{0,4},{4,0},{8,12},{12,8},{16,20},{20,16},{24,28},{28,24},{1,5},{5... | collective-permute-start | bytes 1622024 | tf_op jit(solution)/shard_map/ppermute | solution.py:185
  46.0 22.8 %collective-permute-start.3 = (bf16[176,1536]{1,0:T(8,128)(2,1)S(1)}, bf16[176,1536]{1,0:T(8,128)(2,1)}, u32[]{:S(2)}, u32[]{:S(2)}) collective-permute-start(bf16[176,1536]{1,0:T(8,128)(2,1)S(1)} %collective-permute-done.1.refs_4_), channel_id=1, source_target_pairs={{0,4},{4,0},{8,12},{12,8},{16,20},{20,16},{24,28},{28,24},{1,5},{5... | collective-permute-start | bytes 1622024 | tf_op jit(solution)/shard_map/ppermute | solution.py:185
  46.5 33.9 %collective-permute-start.9 = (bf16[176,1536]{1,0:T(8,128)(2,1)S(1)}, bf16[176,1536]{1,0:T(8,128)(2,1)}, u32[]{:S(2)}, u32[]{:S(2)}) collective-permute-start(bf16[176,1536]{1,0:T(8,128)(2,1)S(1)} %collective-permute-done.7.refs_5_), channel_id=1, source_target_pairs={{0,4},{4,0},{8,12},{12,8},{16,20},{20,16},{24,28},{28,24},{1,5},{5... | collective-permute-start | bytes 1622024 | tf_op jit(solution)/shard_map/ppermute | solution.py:185
  66.0 30.6 %collective-permute-start.8 = (bf16[176,1536]{1,0:T(8,128)(2,1)S(1)}, bf16[176,1536]{1,0:T(8,128)(2,1)}, u32[]{:S(2)}, u32[]{:S(2)}) collective-permute-start(bf16[176,1536]{1,0:T(8,128)(2,1)S(1)} %collective-permute-done.7.refs_5_), channel_id=1, source_target_pairs={{0,1},{1,0},{2,3},{3,2},{4,5},{5,4},{6,7},{7,6},{8,9},{9,8},{10,11... | collective-permute-start | bytes 1622024 | tf_op jit(solution)/shard_map/ppermute | solution.py:185
  68.8 27.7 %collective-permute-start.6 = (bf16[176,1536]{1,0:T(8,128)(2,1)}, bf16[176,1536]{1,0:T(8,128)(2,1)S(1)}, u32[]{:S(2)}, u32[]{:S(2)}) collective-permute-start(bf16[176,1536]{1,0:T(8,128)(2,1)} %collective-permute-done.5.refs_3_), channel_id=1, source_target_pairs={{0,1},{1,0},{2,3},{3,2},{4,5},{5,4},{6,7},{7,6},{8,9},{9,8},{10,11... | collective-permute-start | bytes 1622024 | tf_op jit(solution)/shard_map/ppermute | solution.py:185
  71.1 25.4 %collective-permute-start.4 = (bf16[176,1536]{1,0:T(8,128)(2,1)}, bf16[176,1536]{1,0:T(8,128)(2,1)}, u32[]{:S(2)}, u32[]{:S(2)}) collective-permute-start(bf16[176,1536]{1,0:T(8,128)(2,1)} %collective-permute-done.3.refs_1_), channel_id=1, source_target_pairs={{0,1},{1,0},{2,3},{3,2},{4,5},{5,4},{6,7},{7,6},{8,9},{9,8},{10,11... | collective-permute-start | bytes 1622024 | tf_op jit(solution)/shard_map/ppermute | solution.py:185
  80.4 16.2 %collective-permute-start.15 = (bf16[176,1536]{1,0:T(8,128)(2,1)}, bf16[176,1536]{1,0:T(8,128)(2,1)}, u32[]{:S(2)}, u32[]{:S(2)}) collective-permute-start(bf16[176,1536]{1,0:T(8,128)(2,1)} %collective-permute-done.9.refs_7_), channel_id=1, source_target_pairs={{0,1},{1,0},{2,3},{3,2},{4,5},{5,4},{6,7},{7,6},{8,9},{9,8},{10,11... | collective-permute-start | bytes 1622024 | tf_op jit(solution)/shard_map/ppermute | solution.py:185
  95.2 22.1 %collective-permute-start.16 = (bf16[768,1536]{1,0:T(8,128)(2,1)}, bf16[768,1536]{1,0:T(8,128)(2,1)S(1)}, u32[]{:S(2)}, u32[]{:S(2)}) collective-permute-start(bf16[768,1536]{1,0:T(8,128)(2,1)} %broadcast_select_fusion), channel_id=1, source_target_pairs={{0,1},{2,3},{4,5},{6,7},{9,8},{11,10},{13,12},{15,14},{18,19},{16,... | collective-permute-start | bytes 7077896 | tf_op jit(solution)/shard_map/ppermute | solution.py:185
  96.5 0.8 copy-start.5
  126.9 1.9 copy-start.1
  126.9 60.4 %collective-permute-start.17 = (bf16[768,2560]{1,0:T(8,128)(2,1)S(1)}, bf16[768,2560]{1,0:T(8,128)(2,1)S(1)}, u32[]{:S(2)}, u32[]{:S(2)}) collective-permute-start(bf16[768,2560]{1,0:T(8,128)(2,1)S(1)} %convolution_convert_fusion.lrq_ref), channel_id=1, source_target_pairs={{0,1},{1,0},{2,3},{3,2},{4,5},{5,4},{6,7},{7,6},{8,9},{9,8},{10,11... | collective-permute-start | bytes 11796488 | tf_op jit(solution)/shard_map/ppermute | solution.py:185
  186.1 49.5 %collective-permute-start.18 = (bf16[1536,768]{1,0:T(8,128)(2,1)}, bf16[1536,768]{1,0:T(8,128)(2,1)}, u32[]{:S(2)}, u32[]{:S(2)}) collective-permute-start(bf16[1536,768]{1,0:T(8,128)(2,1)} %convolution_convert_fusion.1), channel_id=1, source_target_pairs={{0,1},{1,0},{2,3},{3,2},{4,5},{5,4},{6,7},{7,6},{8,9},{9,8},{10,11... | collective-permute-start | bytes 7077896 | tf_op jit(solution)/shard_map/ppermute | solution.py:185
  187.3 1.9 copy-start.2
  246.1 2.1 copy-start
  248.4 27.7 %collective-permute-start.19 = (bf16[4,192,768]{2,1,0:T(8,128)(2,1)S(1)}, bf16[4,192,768]{2,1,0:T(8,128)(2,1)S(1)}, u32[]{:S(2)}, u32[]{:S(2)}) collective-permute-start(bf16[4,192,768]{2,1,0:T(8,128)(2,1)S(1)} %fusion.5), channel_id=1, source_target_pairs={{0,2},{1,3},{2,0},{3,1},{4,6},{5,7},{6,4},{7,5},{8,10},{9,11},{10,... | collective-permute-start | bytes 3538952 | tf_op jit(solution)/shard_map/ppermute | solution.py:185
  278.0 28.2 %collective-permute-start.22 = (bf16[192,768]{1,0:T(8,128)(2,1)S(1)}, bf16[192,768]{1,0:T(8,128)(2,1)S(1)}, u32[]{:S(2)}, u32[]{:S(2)}) collective-permute-start(bf16[192,768]{1,0:T(8,128)(2,1)S(1)} %get-tuple-element.63), channel_id=1, source_target_pairs={{0,16},{1,24},{2,20},{3,28},{4,0},{5,8},{6,4},{7,12},{8,17},{9,25}... | collective-permute-start | bytes 884744 | tf_op jit(solution)/shard_map/ppermute | solution.py:185
  278.1 28.1 %collective-permute-start.23 = (bf16[192,768]{1,0:T(8,128)(2,1)S(1)}, bf16[192,768]{1,0:T(8,128)(2,1)S(1)}, u32[]{:S(2)}, u32[]{:S(2)}) collective-permute-start(bf16[192,768]{1,0:T(8,128)(2,1)S(1)} %get-tuple-element.64), channel_id=1, source_target_pairs={{0,24},{1,16},{2,28},{3,20},{4,8},{5,0},{6,12},{7,4},{8,25},{9,17}... | collective-permute-start | bytes 884744 | tf_op jit(solution)/shard_map/ppermute | solution.py:185
  283.2 27.3 %collective-permute-start.21 = (bf16[192,768]{1,0:T(8,128)(2,1)S(1)}, bf16[192,768]{1,0:T(8,128)(2,1)S(1)}, u32[]{:S(2)}, u32[]{:S(2)}) collective-permute-start(bf16[192,768]{1,0:T(8,128)(2,1)S(1)} %get-tuple-element.65), channel_id=1, source_target_pairs={{0,8},{1,0},{2,12},{3,4},{4,24},{5,16},{6,28},{7,20},{8,9},{9,1},{... | collective-permute-start | bytes 884744 | tf_op jit(solution)/shard_map/ppermute | solution.py:185
  284.5 32.1 %collective-permute-start.20 = (bf16[192,768]{1,0:T(8,128)(2,1)S(1)}, bf16[192,768]{1,0:T(8,128)(2,1)S(1)}, u32[]{:S(2)}, u32[]{:S(2)}) collective-permute-start(bf16[192,768]{1,0:T(8,128)(2,1)S(1)} %get-tuple-element.66), channel_id=1, source_target_pairs={{0,0},{1,8},{2,4},{3,12},{4,16},{5,24},{6,20},{7,28},{8,1},{9,9},{... | collective-permute-start | bytes 884744 | tf_op jit(solution)/shard_map/ppermute | solution.py:185

commit v2 on v1

--- a/solution.py
+++ b/solution.py
@@ -229,8 +229,9 @@
     z2, z1, z3 = tie((z2, z1, z3))
     x2 = across(z2)
     near_four = [own] + [h for part in (x0, z1, z3) for h in (part, other(part))]
-    lrp, stack, weight_rows = project(core.reshape(1), near_four, [width] + [occ] * 6, collocation, 2, 0)
-    far_alike, far_unlike, weight_rows = tie((far_alike, far_unlike, weight_rows))
+    side, far_unlike = tie((core.reshape(1), far_unlike))
+    lrp, stack, weight_rows = project(side, near_four, [width] + [occ] * 6, collocation, 2, 0)
+    far_alike, weight_rows = tie((far_alike, weight_rows))
     first = (lrp, stack, weight_rows)
     x2, *first = tie((x2, *first))
     far_four = [h for part in (x1, x3, z2, x2) for h in (part, other(part))]

time: 319 us -> 309 us (0.969)
  starting transfers between devices: 38.5 us -> 29.5 us
    ppermute x24, starting transfers between devices: 38.5 us -> 29.5 us  [send(): return lax.ppermute(x, axes, pairs)]
  transfers between devices with their start and end apart: 24 -> 24, of which waited for: 9 -> 8; matrix products, arithmetic and copies ran while one was open for 6% -> 5% of each run, Pallas kernels for 45% -> 48%
where the time goes in v2:
time: 309 us; the launch traced here: 308 us
  Pallas kernels  147 us (48%)
  waiting for transfers between devices  80.5 us (26%)
  matrix products  31 us (10%)
  starting transfers between devices  29.5 us (10%)
  local copies, waits for them, and re-layouts  10.3 us (3%)
  other arithmetic  7.44 us (2%)
    pallas_call x2, Pallas kernels, pair_gradients(): pl.pallas_call(functools.partial(pair_kernel, sub), out_shape=jax.ShapeDt...  92.8 us
    ppermute x24, waiting for transfers between devices, send(): return lax.ppermute(x, axes, pairs)  80.5 us
    pallas_call x2, Pallas kernels, project(): pl.pallas_call(functools.partial(project_kernel, tuple(rows_each), len(be...  36.5 us
    dot_general x3, matrix products, dot(): return lax.dot_general(a, b, dims, preferred_element_type=F32)  31 us
    ppermute x24, starting transfers between devices, send(): return lax.ppermute(x, axes, pairs)  29.5 us
    pallas_call x1, Pallas kernels, turned(): pl.pallas_call(turn_kernel, out_shape=jax.ShapeDtypeStruct((cols, rows),...  14.7 us
  transfers between devices with their start and end apart: 24, of which 8 were waited for; matrix products, arithmetic and copies ran while one was open for 5% of the time, Pallas kernels for 48%

profile of v2, /device:TPU:19, one launch (start us, length us, event | category | flops | bytes accessed | tf_op | source)
XLA Modules:
  0.0 308.1 jit_solution(11167318938655210220)
XLA Ops:
  0.0 4.1 %constant_dynamic-slice_fusion = (bf16[768,1536]{1,0:T(8,128)(2,1)}, bf16[768,1536]{1,0:T(8,128)(2,1)S(1)}) fusion(bf16[3072,1536]{1,0:T(8,128)(2,1)} %refs_9_.1, s32[]{:T(128)S(6)} %select_n.146, s32[]{:T(128)S(6)} %select_n.145), kind=kLoop, calls=%fused_computation.21 | loop fusion | bytes 9437192 | tf_op jit(solution)/shard_map/dynamic_slice | solution.py:220
  4.1 0.8 collective-permute-start.10
  6.2 2.6 shard_map.73
  8.8 1.8 collective-permute-start.2
  10.5 0.9 collective-permute-start.1
  11.4 0.3 collective-permute-start
  11.7 14.7 %shard_map.74.kt_ref = bf16[1536,3072]{1,0:T(8,128)(2,1)} custom-call(bf16[3072,1536]{1,0:T(8,128)(2,1)} %in_ref.1), custom_call_target="tpu_custom_call" | custom-call | bytes 47185920 | tf_op jit(solution)/shard_map/pallas_call | solution.py:36
  26.3 0.0 collective-permute-done.2.refs_6_
  26.3 7.9 %collective-permute-done.1.refs_4_ = bf16[176,1536]{1,0:T(8,128)(2,1)} collective-permute-done((bf16[176,1536]{1,0:T(8,128)(2,1)}, bf16[176,1536]{1,0:T(8,128)(2,1)}, u32[]{:S(2)}, u32[]{:S(2)}) %collective-permute-start.1) | collective-permute-done | bytes 540704 | tf_op jit(solution)/shard_map/ppermute | solution.py:185
  34.2 0.0 collective-permute-done.refs_2_
  34.2 2.2 collective-permute-start.7
  36.4 0.3 collective-permute-start.5
  36.6 2.1 collective-permute-start.14
  38.7 1.2 collective-permute-start.3
  39.9 10.9 %collective-permute-done.7.refs_5_ = bf16[176,1536]{1,0:T(8,128)(2,1)S(1)} collective-permute-done((bf16[176,1536]{1,0:T(8,128)(2,1)}, bf16[176,1536]{1,0:T(8,128)(2,1)S(1)}, u32[]{:S(2)}, u32[]{:S(2)}) %collective-permute-start.7) | collective-permute-done | bytes 540704 | tf_op jit(solution)/shard_map/ppermute | solution.py:185
  50.8 0.8 collective-permute-start.11
  51.6 0.9 collective-permute-start.12
  52.5 0.0 collective-permute-done.10
  52.5 1.5 copy-done.1
  54.0 0.0 collective-permute-start.13
  54.0 0.0 collective-permute-done.11.refs_3_
  54.0 0.3 collective-permute-start.9
  54.3 7.1 %collective-permute-done.3.refs_1_ = bf16[176,1536]{1,0:T(8,128)(2,1)} collective-permute-done((bf16[176,1536]{1,0:T(8,128)(2,1)}, bf16[176,1536]{1,0:T(8,128)(2,1)}, u32[]{:S(2)}, u32[]{:S(2)}) %collective-permute-start.3) | collective-permute-done | bytes 540704 | tf_op jit(solution)/shard_map/ppermute | solution.py:185
  61.4 2.8 collective-permute-start.8
  64.2 0.0 collective-permute-done.12.refs_5_
  64.2 0.0 collective-permute-start.6
  64.2 0.0 collective-permute-done.13.refs_7_
  64.2 0.5 collective-permute-start.4
  64.7 18.5 %shard_map.75 = (bf16[2560,3072]{1,0:T(8,128)(2,1)}, bf16[2560,1536]{1,0:T(8,128)(2,1)}, f32[16,128]{1,0:T(8,128)}) custom-call(s32[1]{0:T(128)} %bitcast.side_ref.refs_0_.block_ref, bf16[336,1536]{1,0:T(8,128)(2,1)} %get-tuple-element.35.refs_1_, bf16[176,1536]{1,0:T(8,128)(2,1)} %collective-permute-done.refs_2_, ...), custom_call_target="tpu_custom_call" | custom-call | flops 18119393280 | bytes 9437184 | tf_op jit(solution)/shard_map/pallas_call | solution.py:119
  83.3 0.0 collective-permute-done.14
  83.3 0.0 collective-permute-done.9.refs_7_
  83.3 0.1 collective-permute-start.15
  83.4 1.7 broadcast_select_fusion
  85.2 1.3 collective-permute-start.16
  86.5 0.0 collective-permute-done.8.refs_6_
  86.5 0.0 collective-permute-done.4.refs_2_
  86.5 17.9 %shard_map.76 = (bf16[2560,3072]{1,0:T(8,128)(2,1)}, bf16[2560,1536]{1,0:T(8,128)(2,1)}, f32[16,128]{1,0:T(8,128)}) custom-call(s32[1]{0:T(128)} %bitcast.side_ref.refs_0_.block_ref, bf16[176,1536]{1,0:T(8,128)(2,1)} %collective-permute-done.3.refs_1_, ...), custom_call_target="tpu_custom_call", output_to_operand_aliasing={{0}: (10, {}), {1}: (11, {}), {2}: (12, {})} | custom-call | flops 18119393280 | bytes 9437184 | tf_op jit(solution)/shard_map/pallas_call | solution.py:119
  104.5 1.4 slice_reduce_fusion
  105.8 0.6 pad_maximum_fusion.weight_ref
  106.5 9.6 %convolution_convert_fusion.lrq_ref = bf16[768,2560]{1,0:T(8,128)(2,1)S(1)} fusion(bf16[2560,1536]{1,0:T(8,128)(2,1)} %get-tuple-element.47, bf16[768,1536]{1,0:T(8,128)(2,1)S(1)} %collective-permute-done.16, bf16[768,1536]{1,0:T(8,128)(2,1)} %get-tuple-element.59, bf16[768,1536]{1,0:T(8,128)(2,1)} %collective-permute-done.14, pred[]{:T(512)S(6)} %eq.8, ...), kind=kOutput, calls=%fused_computation | convolution fusion | flops 6044123136 | bytes 18874370 | tf_op jit(solution)/shard_map/dot_general | solution.py:22
  116.1 1.4 collective-permute-start.17
  117.4 0.6 copy-done.3
  118.0 46.4 %shard_map.77 = bf16[768,2560]{1,0:T(8,128)(2,1)} custom-call(f32[8]{0:T(128)} %pad_maximum_fusion.weight_ref, s32[1]{0:T(128)} %bitcast.5.block_ref, bf16[1536,3072]{1,0:T(8,128)(2,1)} %shard_map.74.kt_ref, bf16[2560,3072]{1,0:T(8,128)(2,1)} %get-tuple-element.50.lrp_ref, bf16[768,2560]{1,0:T(8,128)(2,1)} %copy-done.3), custom_call_target="tpu_custom_call" | custom-call | flops 38654705664 | bytes 34603008 | tf_op jit(solution)/shard_map/pallas_call | solution.py:166
  164.4 10.9 %convolution_convert_fusion.1 = bf16[1536,768]{1,0:T(8,128)(2,1)} fusion(bf16[2560,1536]{1,0:T(8,128)(2,1)} %get-tuple-element.47, bf16[768,2560]{1,0:T(8,128)(2,1)} %shard_map.77), kind=kOutput, calls=%fused_computation.2 | convolution fusion | flops 6040977408 | bytes 14155776 | tf_op jit(solution)/shard_map/dot_general | solution.py:22
  175.3 1.3 collective-permute-start.18
  176.6 1.9 copy-done.4
  178.4 46.4 %shard_map.78 = bf16[768,2560]{1,0:T(8,128)(2,1)} custom-call(f32[8]{0:T(128)} %pad_maximum_fusion.weight_ref, s32[1]{0:T(128)} %bitcast.side_ref.refs_0_.block_ref, bf16[1536,3072]{1,0:T(8,128)(2,1)} %shard_map.74.kt_ref, bf16[2560,3072]{1,0:T(8,128)(2,1)} %get-tuple-element.50.lrp_ref, bf16[768,2560]{1,0:T(8,128)(2,1)} %copy-done.4), custom_call_target="tpu_custom_call" | custom-call | flops 38654705664 | bytes 34603008 | tf_op jit(solution)/shard_map/pallas_call | solution.py:166
  224.9 10.5 %convert_add_fusion = f32[1536,768]{1,0:T(8,128)S(1)} fusion(bf16[1536,768]{1,0:T(8,128)(2,1)} %collective-permute-done.18, bf16[2560,1536]{1,0:T(8,128)(2,1)} %get-tuple-element.47, bf16[768,2560]{1,0:T(8,128)(2,1)} %shard_map.78), kind=kOutput, calls=%fused_computation.1 | convolution fusion | flops 6042157056 | bytes 18874368 | tf_op jit(solution)/shard_map/dot_general | solution.py:22
  235.4 2.1 copy-done
  237.5 0.1 fusion.5
  237.6 2.3 collective-permute-start.19
  239.9 26.3 %collective-permute-done.19 = bf16[4,192,768]{2,1,0:T(8,128)(2,1)S(1)} collective-permute-done((bf16[4,192,768]{2,1,0:T(8,128)(2,1)S(1)}, bf16[4,192,768]{2,1,0:T(8,128)(2,1)S(1)}, u32[]{:S(2)}, u32[]{:S(2)}) %collective-permute-start.19) | collective-permute-done | bytes 1179680 | tf_op jit(solution)/shard_map/ppermute | solution.py:185
  266.2 1.9 fusion
  268.2 0.1 dynamic-slice_bitcast_fusion.1
  268.3 1.3 collective-permute-start.22
  269.6 3.7 %collective-permute-start.23 = (bf16[192,768]{1,0:T(8,128)(2,1)S(1)}, bf16[192,768]{1,0:T(8,128)(2,1)S(1)}, u32[]{:S(2)}, u32[]{:S(2)}) collective-permute-start(bf16[192,768]{1,0:T(8,128)(2,1)S(1)} %get-tuple-element.66), channel_id=1, source_target_pairs={{0,24},{1,16},{2,28},{3,20},{4,8},{5,0},{6,12},{7,4},{8,25},{9,17}... | collective-permute-start | bytes 884744 | tf_op jit(solution)/shard_map/ppermute | solution.py:185
  273.2 1.0 collective-permute-start.21
  274.2 2.4 collective-permute-start.20
  278.0 16.7 %collective-permute-done.22 = bf16[192,768]{1,0:T(8,128)(2,1)S(1)} collective-permute-done((bf16[192,768]{1,0:T(8,128)(2,1)S(1)}, bf16[192,768]{1,0:T(8,128)(2,1)S(1)}, u32[]{:S(2)}, u32[]{:S(2)}) %collective-permute-start.22) | collective-permute-done | bytes 294944 | tf_op jit(solution)/shard_map/ppermute | solution.py:185
  294.7 3.8 %collective-permute-done.23 = bf16[192,768]{1,0:T(8,128)(2,1)S(1)} collective-permute-done((bf16[192,768]{1,0:T(8,128)(2,1)S(1)}, bf16[192,768]{1,0:T(8,128)(2,1)S(1)}, u32[]{:S(2)}, u32[]{:S(2)}) %collective-permute-start.23) | collective-permute-done | bytes 294944 | tf_op jit(solution)/shard_map/ppermute | solution.py:185
  298.4 0.9 collective-permute-done.21
  299.4 6.9 %collective-permute-done.20 = bf16[192,768]{1,0:T(8,128)(2,1)S(1)} collective-permute-done((bf16[192,768]{1,0:T(8,128)(2,1)S(1)}, bf16[192,768]{1,0:T(8,128)(2,1)S(1)}, u32[]{:S(2)}, u32[]{:S(2)}) %collective-permute-start.20) | collective-permute-done | bytes 294944 | tf_op jit(solution)/shard_map/ppermute | solution.py:185
  306.3 0.1 select_select_fusion.3
  306.5 1.7 divide_bitcast_fusion
  (16 shorter events, 0.0 us)
Async XLA Ops:
  4.1 48.4 %collective-permute-start.10 = (bf16[768,1536]{1,0:T(8,128)(2,1)S(1)}, bf16[768,1536]{1,0:T(8,128)(2,1)S(1)}, u32[]{:S(2)}, u32[]{:S(2)}) collective-permute-start(bf16[768,1536]{1,0:T(8,128)(2,1)S(1)} %get-tuple-element.60), channel_id=1, source_target_pairs={{0,2},{4,6},{9,11},{13,15},{18,16},{22,20},{27,25},{31,29}} | collective-permute-start | bytes 7077896 | tf_op jit(solution)/shard_map/ppermute | solution.py:185
  8.8 17.6 %collective-permute-start.2 = (bf16[176,1536]{1,0:T(8,128)(2,1)}, bf16[176,1536]{1,0:T(8,128)(2,1)}, u32[]{:S(2)}, u32[]{:S(2)}) collective-permute-start(bf16[176,1536]{1,0:T(8,128)(2,1)} %get-tuple-element.30), channel_id=1, source_target_pairs={{0,8},{4,12},{8,16},{12,20},{16,24},{20,28},{24,0},{28,4},{1,9},{5... | collective-permute-start | bytes 1622024 | tf_op jit(solution)/shard_map/ppermute | solution.py:185
  10.5 23.7 %collective-permute-start.1 = (bf16[176,1536]{1,0:T(8,128)(2,1)}, bf16[176,1536]{1,0:T(8,128)(2,1)}, u32[]{:S(2)}, u32[]{:S(2)}) collective-permute-start(bf16[176,1536]{1,0:T(8,128)(2,1)} %get-tuple-element.30), channel_id=1, source_target_pairs={{0,24},{4,28},{8,0},{12,4},{16,8},{20,12},{24,16},{28,20},{1,25},{... | collective-permute-start | bytes 1622024 | tf_op jit(solution)/shard_map/ppermute | solution.py:185
  11.4 22.8 %collective-permute-start = (bf16[176,1536]{1,0:T(8,128)(2,1)}, bf16[176,1536]{1,0:T(8,128)(2,1)}, u32[]{:S(2)}, u32[]{:S(2)}) collective-permute-start(bf16[176,1536]{1,0:T(8,128)(2,1)} %get-tuple-element.30), channel_id=1, source_target_pairs={{0,4},{4,0},{8,12},{12,8},{16,20},{20,16},{24,28},{28,24},{1,5},{5... | collective-permute-start | bytes 1622024 | tf_op jit(solution)/shard_map/ppermute | solution.py:185
  34.2 16.6 %collective-permute-start.7 = (bf16[176,1536]{1,0:T(8,128)(2,1)}, bf16[176,1536]{1,0:T(8,128)(2,1)S(1)}, u32[]{:S(2)}, u32[]{:S(2)}) collective-permute-start(bf16[176,1536]{1,0:T(8,128)(2,1)} %collective-permute-done.1.refs_4_), channel_id=1, source_target_pairs={{0,24},{4,28},{8,0},{12,4},{16,8},{20,12},{24,16},{28,20},{1,25},{... | collective-permute-start | bytes 1622024 | tf_op jit(solution)/shard_map/ppermute | solution.py:185
  36.4 15.2 %collective-permute-start.5 = (bf16[176,1536]{1,0:T(8,128)(2,1)}, bf16[176,1536]{1,0:T(8,128)(2,1)S(1)}, u32[]{:S(2)}, u32[]{:S(2)}) collective-permute-start(bf16[176,1536]{1,0:T(8,128)(2,1)} %collective-permute-done.2.refs_6_), channel_id=1, source_target_pairs={{0,4},{4,0},{8,12},{12,8},{16,20},{20,16},{24,28},{28,24},{1,5},{5... | collective-permute-start | bytes 1622024 | tf_op jit(solution)/shard_map/ppermute | solution.py:185
  36.6 46.6 %collective-permute-start.14 = (bf16[768,1536]{1,0:T(8,128)(2,1)}, bf16[768,1536]{1,0:T(8,128)(2,1)}, u32[]{:S(2)}, u32[]{:S(2)}) collective-permute-start(bf16[768,1536]{1,0:T(8,128)(2,1)} %get-tuple-element.59), channel_id=1, source_target_pairs={{0,2},{4,6},{9,11},{13,15},{18,16},{22,20},{27,25},{31,29}} | collective-permute-start | bytes 7077896 | tf_op jit(solution)/shard_map/ppermute | solution.py:185
  38.7 22.6 %collective-permute-start.3 = (bf16[176,1536]{1,0:T(8,128)(2,1)}, bf16[176,1536]{1,0:T(8,128)(2,1)}, u32[]{:S(2)}, u32[]{:S(2)}) collective-permute-start(bf16[176,1536]{1,0:T(8,128)(2,1)} %collective-permute-done.1.refs_4_), channel_id=1, source_target_pairs={{0,4},{4,0},{8,12},{12,8},{16,20},{20,16},{24,28},{28,24},{1,5},{5... | collective-permute-start | bytes 1622024 | tf_op jit(solution)/shard_map/ppermute | solution.py:185
  50.8 32.5 %copy-start.5 = (bf16[176,1536]{1,0:T(8,128)(2,1)}, bf16[176,1536]{1,0:T(8,128)(2,1)S(1)}, u32[]{:S(2)}) copy-start(bf16[176,1536]{1,0:T(8,128)(2,1)S(1)} %collective-permute-done.7.refs_5_) | copy-start | bytes 1622020
  50.8 3.2 %collective-permute-start.11 = (bf16[176,1536]{1,0:T(8,128)(2,1)}, bf16[176,1536]{1,0:T(8,128)(2,1)}, u32[]{:S(2)}, u32[]{:S(2)}) collective-permute-start(bf16[176,1536]{1,0:T(8,128)(2,1)} %collective-permute-done.refs_2_), channel_id=1, source_target_pairs={{0,1},{1,0},{2,3},{3,2},{4,5},{5,4},{6,7},{7,6},{8,9},{9,8},{10,11... | collective-permute-start | bytes 1622024 | tf_op jit(solution)/shard_map/ppermute | solution.py:185
  51.6 31.7 %copy-start.6 = (bf16[176,1536]{1,0:T(8,128)(2,1)}, bf16[176,1536]{1,0:T(8,128)(2,1)S(1)}, u32[]{:S(2)}) copy-start(bf16[176,1536]{1,0:T(8,128)(2,1)S(1)} %collective-permute-done.5.refs_3_) | copy-start | bytes 1622020
  51.6 12.6 %collective-permute-start.12 = (bf16[176,1536]{1,0:T(8,128)(2,1)}, bf16[176,1536]{1,0:T(8,128)(2,1)}, u32[]{:S(2)}, u32[]{:S(2)}) collective-permute-start(bf16[176,1536]{1,0:T(8,128)(2,1)} %collective-permute-done.1.refs_4_), channel_id=1, source_target_pairs={{0,1},{1,0},{2,3},{3,2},{4,5},{5,4},{6,7},{7,6},{8,9},{9,8},{10,11... | collective-permute-start | bytes 1622024 | tf_op jit(solution)/shard_map/ppermute | solution.py:185
  52.5 1.5 copy-start.1
  54.0 10.2 %collective-permute-start.13 = (bf16[176,1536]{1,0:T(8,128)(2,1)}, bf16[176,1536]{1,0:T(8,128)(2,1)}, u32[]{:S(2)}, u32[]{:S(2)}) collective-permute-start(bf16[176,1536]{1,0:T(8,128)(2,1)} %collective-permute-done.2.refs_6_), channel_id=1, source_target_pairs={{0,1},{1,0},{2,3},{3,2},{4,5},{5,4},{6,7},{7,6},{8,9},{9,8},{10,11... | collective-permute-start | bytes 1622024 | tf_op jit(solution)/shard_map/ppermute | solution.py:185
  54.0 29.3 %collective-permute-start.9 = (bf16[176,1536]{1,0:T(8,128)(2,1)S(1)}, bf16[176,1536]{1,0:T(8,128)(2,1)}, u32[]{:S(2)}, u32[]{:S(2)}) collective-permute-start(bf16[176,1536]{1,0:T(8,128)(2,1)S(1)} %collective-permute-done.7.refs_5_), channel_id=1, source_target_pairs={{0,4},{4,0},{8,12},{12,8},{16,20},{20,16},{24,28},{28,24},{1,5},{5... | collective-permute-start | bytes 1622024 | tf_op jit(solution)/shard_map/ppermute | solution.py:185
  61.4 25.1 %collective-permute-start.8 = (bf16[176,1536]{1,0:T(8,128)(2,1)S(1)}, bf16[176,1536]{1,0:T(8,128)(2,1)}, u32[]{:S(2)}, u32[]{:S(2)}) collective-permute-start(bf16[176,1536]{1,0:T(8,128)(2,1)S(1)} %collective-permute-done.7.refs_5_), channel_id=1, source_target_pairs={{0,1},{1,0},{2,3},{3,2},{4,5},{5,4},{6,7},{7,6},{8,9},{9,8},{10,11... | collective-permute-start | bytes 1622024 | tf_op jit(solution)/shard_map/ppermute | solution.py:185
  64.2 22.3 %collective-permute-start.6 = (bf16[176,1536]{1,0:T(8,128)(2,1)S(1)}, bf16[176,1536]{1,0:T(8,128)(2,1)}, u32[]{:S(2)}, u32[]{:S(2)}) collective-permute-start(bf16[176,1536]{1,0:T(8,128)(2,1)S(1)} %collective-permute-done.5.refs_3_), channel_id=1, source_target_pairs={{0,1},{1,0},{2,3},{3,2},{4,5},{5,4},{6,7},{7,6},{8,9},{9,8},{10,11... | collective-permute-start | bytes 1622024 | tf_op jit(solution)/shard_map/ppermute | solution.py:185
  64.2 22.3 %collective-permute-start.4 = (bf16[176,1536]{1,0:T(8,128)(2,1)}, bf16[176,1536]{1,0:T(8,128)(2,1)}, u32[]{:S(2)}, u32[]{:S(2)}) collective-permute-start(bf16[176,1536]{1,0:T(8,128)(2,1)} %collective-permute-done.3.refs_1_), channel_id=1, source_target_pairs={{0,1},{1,0},{2,3},{3,2},{4,5},{5,4},{6,7},{7,6},{8,9},{9,8},{10,11... | collective-permute-start | bytes 1622024 | tf_op jit(solution)/shard_map/ppermute | solution.py:185
  64.7 18.7 %copy-start.2 = (bf16[768,1536]{1,0:T(8,128)(2,1)S(1)}, bf16[768,1536]{1,0:T(8,128)(2,1)}, u32[]{:S(2)}) copy-start(bf16[768,1536]{1,0:T(8,128)(2,1)} %copy-done.1) | copy-start | bytes 7077892
  83.3 3.2 %collective-permute-start.15 = (bf16[176,1536]{1,0:T(8,128)(2,1)}, bf16[176,1536]{1,0:T(8,128)(2,1)}, u32[]{:S(2)}, u32[]{:S(2)}) collective-permute-start(bf16[176,1536]{1,0:T(8,128)(2,1)} %collective-permute-done.9.refs_7_), channel_id=1, source_target_pairs={{0,1},{1,0},{2,3},{3,2},{4,5},{5,4},{6,7},{7,6},{8,9},{9,8},{10,11... | collective-permute-start | bytes 1622024 | tf_op jit(solution)/shard_map/ppermute | solution.py:185
  85.2 21.3 %collective-permute-start.16 = (bf16[768,1536]{1,0:T(8,128)(2,1)}, bf16[768,1536]{1,0:T(8,128)(2,1)S(1)}, u32[]{:S(2)}, u32[]{:S(2)}) collective-permute-start(bf16[768,1536]{1,0:T(8,128)(2,1)} %broadcast_select_fusion), channel_id=1, source_target_pairs={{0,1},{2,3},{4,5},{6,7},{9,8},{11,10},{13,12},{15,14},{18,19},{16,... | collective-permute-start | bytes 7077896 | tf_op jit(solution)/shard_map/ppermute | solution.py:185
  116.1 1.9 copy-start.3
  116.1 60.5 %collective-permute-start.17 = (bf16[768,2560]{1,0:T(8,128)(2,1)S(1)}, bf16[768,2560]{1,0:T(8,128)(2,1)S(1)}, u32[]{:S(2)}, u32[]{:S(2)}) collective-permute-start(bf16[768,2560]{1,0:T(8,128)(2,1)S(1)} %convolution_convert_fusion.lrq_ref), channel_id=1, source_target_pairs={{0,1},{1,0},{2,3},{3,2},{4,5},{5,4},{6,7},{7,6},{8,9},{9,8},{10,11... | collective-permute-start | bytes 11796488 | tf_op jit(solution)/shard_map/ppermute | solution.py:185
  175.3 49.6 %collective-permute-start.18 = (bf16[1536,768]{1,0:T(8,128)(2,1)}, bf16[1536,768]{1,0:T(8,128)(2,1)}, u32[]{:S(2)}, u32[]{:S(2)}) collective-permute-start(bf16[1536,768]{1,0:T(8,128)(2,1)} %convolution_convert_fusion.1), channel_id=1, source_target_pairs={{0,1},{1,0},{2,3},{3,2},{4,5},{5,4},{6,7},{7,6},{8,9},{9,8},{10,11... | collective-permute-start | bytes 7077896 | tf_op jit(solution)/shard_map/ppermute | solution.py:185
  176.6 1.9 copy-start.4
  235.4 2.1 copy-start
  237.6 28.6 %collective-permute-start.19 = (bf16[4,192,768]{2,1,0:T(8,128)(2,1)S(1)}, bf16[4,192,768]{2,1,0:T(8,128)(2,1)S(1)}, u32[]{:S(2)}, u32[]{:S(2)}) collective-permute-start(bf16[4,192,768]{2,1,0:T(8,128)(2,1)S(1)} %fusion.5), channel_id=1, source_target_pairs={{0,2},{1,3},{2,0},{3,1},{4,6},{5,7},{6,4},{7,5},{8,10},{9,11},{10,... | collective-permute-start | bytes 3538952 | tf_op jit(solution)/shard_map/ppermute | solution.py:185
  268.3 26.4 %collective-permute-start.22 = (bf16[192,768]{1,0:T(8,128)(2,1)S(1)}, bf16[192,768]{1,0:T(8,128)(2,1)S(1)}, u32[]{:S(2)}, u32[]{:S(2)}) collective-permute-start(bf16[192,768]{1,0:T(8,128)(2,1)S(1)} %get-tuple-element.65), channel_id=1, source_target_pairs={{0,16},{1,24},{2,20},{3,28},{4,0},{5,8},{6,4},{7,12},{8,17},{9,25}... | collective-permute-start | bytes 884744 | tf_op jit(solution)/shard_map/ppermute | solution.py:185
  269.6 28.9 %collective-permute-start.23 = (bf16[192,768]{1,0:T(8,128)(2,1)S(1)}, bf16[192,768]{1,0:T(8,128)(2,1)S(1)}, u32[]{:S(2)}, u32[]{:S(2)}) collective-permute-start(bf16[192,768]{1,0:T(8,128)(2,1)S(1)} %get-tuple-element.66), channel_id=1, source_target_pairs={{0,24},{1,16},{2,28},{3,20},{4,8},{5,0},{6,12},{7,4},{8,25},{9,17}... | collective-permute-start | bytes 884744 | tf_op jit(solution)/shard_map/ppermute | solution.py:185
  273.2 26.1 %collective-permute-start.21 = (bf16[192,768]{1,0:T(8,128)(2,1)S(1)}, bf16[192,768]{1,0:T(8,128)(2,1)S(1)}, u32[]{:S(2)}, u32[]{:S(2)}) collective-permute-start(bf16[192,768]{1,0:T(8,128)(2,1)S(1)} %get-tuple-element.67), channel_id=1, source_target_pairs={{0,8},{1,0},{2,12},{3,4},{4,24},{5,16},{6,28},{7,20},{8,9},{9,1},{... | collective-permute-start | bytes 884744 | tf_op jit(solution)/shard_map/ppermute | solution.py:185
  274.2 32.1 %collective-permute-start.20 = (bf16[192,768]{1,0:T(8,128)(2,1)S(1)}, bf16[192,768]{1,0:T(8,128)(2,1)S(1)}, u32[]{:S(2)}, u32[]{:S(2)}) collective-permute-start(bf16[192,768]{1,0:T(8,128)(2,1)S(1)} %get-tuple-element.68), channel_id=1, source_target_pairs={{0,0},{1,8},{2,4},{3,12},{4,16},{5,24},{6,20},{7,28},{8,1},{9,9},{... | collective-permute-start | bytes 884744 | tf_op jit(solution)/shard_map/ppermute | solution.py:185

commit v3 on v2

--- a/solution.py
+++ b/solution.py
@@ -233,7 +233,7 @@
     lrp, stack, weight_rows = project(side, near_four, [width] + [occ] * 6, collocation, 2, 0)
     far_alike, weight_rows = tie((far_alike, weight_rows))
     first = (lrp, stack, weight_rows)
-    x2, *first = tie((x2, *first))
+    x1, x3, x2, *first = tie((x1, x3, x2, *first))
     far_four = [h for part in (x1, x3, z2, x2) for h in (part, other(part))]
     lrp, stack, weight_rows = project(core.reshape(1), far_four, [occ] * 8, collocation, 2, 1, first)
     weights = jnp.concatenate([weight_rows[:4, 0], weight_rows[8:12, 0]])

time: 309 us -> 317 us (1.026)
  waiting for transfers between devices: 80.5 us -> 93.1 us
  starting transfers between devices: 29.5 us -> 25.8 us
    ppermute x24, waiting for transfers between devices: 80.5 us -> 93.1 us  [send(): return lax.ppermute(x, axes, pairs)]
    ppermute x24, starting transfers between devices: 29.5 us -> 25.8 us  [send(): return lax.ppermute(x, axes, pairs)]
  transfers between devices with their start and end apart: 24 -> 24, of which waited for: 8 -> 10; matrix products, arithmetic and copies ran while one was open for 5% -> 5% of each run, Pallas kernels for 48% -> 46%
where the time goes in v3:
time: 317 us
  Pallas kernels  146 us (46%)
  waiting for transfers between devices  93.1 us (29%)
  matrix products  31 us (10%)
  starting transfers between devices  25.8 us (8%)
  other arithmetic  9.02 us (3%)
  local copies, waits for them, and re-layouts  8.86 us (3%)
    ppermute x24, waiting for transfers between devices, send(): return lax.ppermute(x, axes, pairs)  93.1 us
    pallas_call x2, Pallas kernels, pair_gradients(): pl.pallas_call(functools.partial(pair_kernel, sub), out_shape=jax.ShapeDt...  92.7 us
    pallas_call x2, Pallas kernels, project(): pl.pallas_call(functools.partial(project_kernel, tuple(rows_each), len(be...  36.3 us
    dot_general x3, matrix products, dot(): return lax.dot_general(a, b, dims, preferred_element_type=F32)  31 us
    ppermute x24, starting transfers between devices, send(): return lax.ppermute(x, axes, pairs)  25.8 us
    pallas_call x1, Pallas kernels, turned(): pl.pallas_call(turn_kernel, out_shape=jax.ShapeDtypeStruct((cols, rows),...  14.8 us
  transfers between devices with their start and end apart: 24, of which 10 were waited for; matrix products, arithmetic and copies ran while one was open for 5% of the time, Pallas kernels for 46%

profile of v3, /device:TPU:19, one launch (start us, length us, event | category | flops | bytes accessed | tf_op | source)
XLA Modules:
  0.0 316.8 jit_solution(5084377853344752721)
XLA Ops:
  0.0 4.1 %constant_dynamic-slice_fusion = (bf16[768,1536]{1,0:T(8,128)(2,1)}, bf16[768,1536]{1,0:T(8,128)(2,1)S(1)}) fusion(bf16[3072,1536]{1,0:T(8,128)(2,1)} %refs_9_.1, s32[]{:T(128)S(6)} %select_n.146, s32[]{:T(128)S(6)} %select_n.145), kind=kLoop, calls=%fused_computation.21 | loop fusion | bytes 9437192 | tf_op jit(solution)/shard_map/dynamic_slice | solution.py:220
  4.1 2.1 collective-permute-start.7
  7.5 2.6 shard_map.73
  10.1 0.5 collective-permute-start.2
  10.5 2.2 collective-permute-start.1
  12.7 0.3 collective-permute-start
  13.0 14.8 %shard_map.74.kt_ref = bf16[1536,3072]{1,0:T(8,128)(2,1)} custom-call(bf16[3072,1536]{1,0:T(8,128)(2,1)} %in_ref.1), custom_call_target="tpu_custom_call" | custom-call | bytes 47185920 | tf_op jit(solution)/shard_map/pallas_call | solution.py:36
  27.8 0.0 collective-permute-done.2.refs_6_
  27.8 7.3 %collective-permute-done.1.refs_4_ = bf16[176,1536]{1,0:T(8,128)(2,1)} collective-permute-done((bf16[176,1536]{1,0:T(8,128)(2,1)}, bf16[176,1536]{1,0:T(8,128)(2,1)}, u32[]{:S(2)}, u32[]{:S(2)}) %collective-permute-start.1) | collective-permute-done | bytes 540704 | tf_op jit(solution)/shard_map/ppermute | solution.py:185
  35.1 2.2 collective-permute-start.5
  37.2 2.1 collective-permute-start.11
  39.3 0.0 collective-permute-start.8
  39.3 12.8 %collective-permute-done.5.refs_5_ = bf16[176,1536]{1,0:T(8,128)(2,1)S(1)} collective-permute-done((bf16[176,1536]{1,0:T(8,128)(2,1)}, bf16[176,1536]{1,0:T(8,128)(2,1)S(1)}, u32[]{:S(2)}, u32[]{:S(2)}) %collective-permute-start.5) | collective-permute-done | bytes 540704 | tf_op jit(solution)/shard_map/ppermute | solution.py:185
  52.1 0.8 collective-permute-start.9
  52.9 0.0 collective-permute-start.10
  53.0 0.0 collective-permute-done.7
  53.0 0.3 collective-permute-start.4
  53.2 0.0 collective-permute-done.8.refs_3_
  53.2 1.2 collective-permute-start.3
  54.4 0.4 collective-permute-done.9.refs_5_
  54.9 0.6 collective-permute-start.14
  55.5 0.1 collective-permute-done.10.refs_7_
  55.6 0.3 collective-permute-start.6
  55.9 18.4 %shard_map.75 = (bf16[2560,3072]{1,0:T(8,128)(2,1)}, bf16[2560,1536]{1,0:T(8,128)(2,1)}, f32[16,128]{1,0:T(8,128)}) custom-call(s32[1]{0:T(128)} %bitcast.side_ref.refs_0_.block_ref, bf16[336,1536]{1,0:T(8,128)(2,1)} %get-tuple-element.37.refs_1_, bf16[176,1536]{1,0:T(8,128)(2,1)} %collective-permute-done.refs_2_, ...), custom_call_target="tpu_custom_call" | custom-call | flops 18119393280 | bytes 9437184 | tf_op jit(solution)/shard_map/pallas_call | solution.py:119
  74.3 0.0 collective-permute-done.11
  74.3 3.8 %collective-permute-done.3.refs_1_ = bf16[176,1536]{1,0:T(8,128)(2,1)} collective-permute-done((bf16[176,1536]{1,0:T(8,128)(2,1)}, bf16[176,1536]{1,0:T(8,128)(2,1)}, u32[]{:S(2)}, u32[]{:S(2)}) %collective-permute-start.3) | collective-permute-done | bytes 540704 | tf_op jit(solution)/shard_map/ppermute | solution.py:185
  78.2 11.6 %collective-permute-done.6.refs_7_ = bf16[176,1536]{1,0:T(8,128)(2,1)} collective-permute-done((bf16[176,1536]{1,0:T(8,128)(2,1)S(1)}, bf16[176,1536]{1,0:T(8,128)(2,1)}, u32[]{:S(2)}, u32[]{:S(2)}) %collective-permute-start.6) | collective-permute-done | bytes 540704 | tf_op jit(solution)/shard_map/ppermute | solution.py:185
  89.8 1.4 collective-permute-start.12
  91.1 0.0 collective-permute-start.13
  91.1 0.5 collective-permute-start.15
  91.6 3.3 %broadcast_select_fusion = bf16[768,1536]{1,0:T(8,128)(2,1)} fusion(bf16[768,1536]{1,0:T(8,128)(2,1)S(1)} %get-tuple-element.64, bf16[768,1536]{1,0:T(8,128)(2,1)} %collective-permute-done.7, pred[]{:T(512)S(6)} %eq.8), kind=kLoop, calls=%fused_computation.10 | loop fusion | flops 1179648 | bytes 7077889 | tf_op jit(solution)/shard_map/jit(_where)/select_n | solution.py:242
  95.0 1.3 collective-permute-start.16
  96.3 0.0 collective-permute-done.14.refs_6_
  96.3 0.0 collective-permute-done.15.refs_8_
  96.3 17.9 %shard_map.76 = (bf16[2560,3072]{1,0:T(8,128)(2,1)}, bf16[2560,1536]{1,0:T(8,128)(2,1)}, f32[16,128]{1,0:T(8,128)}) custom-call(s32[1]{0:T(128)} %bitcast.side_ref.refs_0_.block_ref, bf16[176,1536]{1,0:T(8,128)(2,1)} %collective-permute-done.3.refs_1_, ...), custom_call_target="tpu_custom_call", output_to_operand_aliasing={{0}: (10, {}), {1}: (11, {}), {2}: (12, {})} | custom-call | flops 18119393280 | bytes 9437184 | tf_op jit(solution)/shard_map/pallas_call | solution.py:119
  114.2 1.3 slice_reduce_fusion
  115.5 0.7 pad_maximum_fusion.weight_ref
  116.2 0.0 collective-permute-done.16
  116.2 9.6 %convolution_convert_fusion.lrq_ref = bf16[768,2560]{1,0:T(8,128)(2,1)S(1)} fusion(bf16[2560,1536]{1,0:T(8,128)(2,1)} %get-tuple-element.51, bf16[768,1536]{1,0:T(8,128)(2,1)S(1)} %collective-permute-done.16, bf16[768,1536]{1,0:T(8,128)(2,1)} %get-tuple-element.63, bf16[768,1536]{1,0:T(8,128)(2,1)} %collective-permute-done.11, pred[]{:T(512)S(6)} %eq.8, ...), kind=kOutput, calls=%fused_computation | convolution fusion | flops 6044123136 | bytes 18874370 | tf_op jit(solution)/shard_map/dot_general | solution.py:22
  125.9 1.3 collective-permute-start.17
  127.2 0.6 copy-done.1
  127.8 46.3 %shard_map.77 = bf16[768,2560]{1,0:T(8,128)(2,1)} custom-call(f32[8]{0:T(128)} %pad_maximum_fusion.weight_ref, s32[1]{0:T(128)} %bitcast.5.block_ref, bf16[1536,3072]{1,0:T(8,128)(2,1)} %shard_map.74.kt_ref, bf16[2560,3072]{1,0:T(8,128)(2,1)} %get-tuple-element.54.lrp_ref, bf16[768,2560]{1,0:T(8,128)(2,1)} %copy-done.1), custom_call_target="tpu_custom_call" | custom-call | flops 38654705664 | bytes 34603008 | tf_op jit(solution)/shard_map/pallas_call | solution.py:166
  174.1 10.9 %convolution_convert_fusion.1 = bf16[1536,768]{1,0:T(8,128)(2,1)} fusion(bf16[2560,1536]{1,0:T(8,128)(2,1)} %get-tuple-element.51, bf16[768,2560]{1,0:T(8,128)(2,1)} %shard_map.77), kind=kOutput, calls=%fused_computation.2 | convolution fusion | flops 6040977408 | bytes 14155776 | tf_op jit(solution)/shard_map/dot_general | solution.py:22
  185.0 1.3 collective-permute-start.18
  186.2 0.0 collective-permute-done.17.lrq_ref
  186.2 1.9 copy-done.2
  188.1 46.4 %shard_map.78 = bf16[768,2560]{1,0:T(8,128)(2,1)} custom-call(f32[8]{0:T(128)} %pad_maximum_fusion.weight_ref, s32[1]{0:T(128)} %bitcast.side_ref.refs_0_.block_ref, bf16[1536,3072]{1,0:T(8,128)(2,1)} %shard_map.74.kt_ref, bf16[2560,3072]{1,0:T(8,128)(2,1)} %get-tuple-element.54.lrp_ref, bf16[768,2560]{1,0:T(8,128)(2,1)} %copy-done.2), custom_call_target="tpu_custom_call" | custom-call | flops 38654705664 | bytes 34603008 | tf_op jit(solution)/shard_map/pallas_call | solution.py:166
  234.5 0.0 collective-permute-done.18
  234.5 10.5 %convert_add_fusion = f32[1536,768]{1,0:T(8,128)S(1)} fusion(bf16[1536,768]{1,0:T(8,128)(2,1)} %collective-permute-done.18, bf16[2560,1536]{1,0:T(8,128)(2,1)} %get-tuple-element.51, bf16[768,2560]{1,0:T(8,128)(2,1)} %shard_map.78), kind=kOutput, calls=%fused_computation.1 | convolution fusion | flops 6042157056 | bytes 18874368 | tf_op jit(solution)/shard_map/dot_general | solution.py:22
  245.0 2.1 copy-done
  247.2 0.1 fusion.5
  247.3 0.5 collective-permute-start.19
  247.8 27.2 %collective-permute-done.19 = bf16[4,192,768]{2,1,0:T(8,128)(2,1)S(1)} collective-permute-done((bf16[4,192,768]{2,1,0:T(8,128)(2,1)S(1)}, bf16[4,192,768]{2,1,0:T(8,128)(2,1)S(1)}, u32[]{:S(2)}, u32[]{:S(2)}) %collective-permute-start.19) | collective-permute-done | bytes 1179680 | tf_op jit(solution)/shard_map/ppermute | solution.py:185
  274.9 1.9 fusion
  276.9 0.1 dynamic-slice_bitcast_fusion.1
  277.0 1.2 collective-permute-start.22
  278.1 4.0 %collective-permute-start.23 = (bf16[192,768]{1,0:T(8,128)(2,1)S(1)}, bf16[192,768]{1,0:T(8,128)(2,1)S(1)}, u32[]{:S(2)}, u32[]{:S(2)}) collective-permute-start(bf16[192,768]{1,0:T(8,128)(2,1)S(1)} %get-tuple-element.70), channel_id=1, source_target_pairs={{0,24},{1,16},{2,28},{3,20},{4,8},{5,0},{6,12},{7,4},{8,25},{9,17}... | collective-permute-start | bytes 884744 | tf_op jit(solution)/shard_map/ppermute | solution.py:185
  282.1 0.0 collective-permute-start.21
  282.1 1.9 collective-permute-start.20
  285.2 16.7 %collective-permute-done.22 = bf16[192,768]{1,0:T(8,128)(2,1)S(1)} collective-permute-done((bf16[192,768]{1,0:T(8,128)(2,1)S(1)}, bf16[192,768]{1,0:T(8,128)(2,1)S(1)}, u32[]{:S(2)}, u32[]{:S(2)}) %collective-permute-start.22) | collective-permute-done | bytes 294944 | tf_op jit(solution)/shard_map/ppermute | solution.py:185
  301.9 7.4 %collective-permute-done.23 = bf16[192,768]{1,0:T(8,128)(2,1)S(1)} collective-permute-done((bf16[192,768]{1,0:T(8,128)(2,1)S(1)}, bf16[192,768]{1,0:T(8,128)(2,1)S(1)}, u32[]{:S(2)}, u32[]{:S(2)}) %collective-permute-start.23) | collective-permute-done | bytes 294944 | tf_op jit(solution)/shard_map/ppermute | solution.py:185
  309.3 5.7 %collective-permute-done.20 = bf16[192,768]{1,0:T(8,128)(2,1)S(1)} collective-permute-done((bf16[192,768]{1,0:T(8,128)(2,1)S(1)}, bf16[192,768]{1,0:T(8,128)(2,1)S(1)}, u32[]{:S(2)}, u32[]{:S(2)}) %collective-permute-start.20) | collective-permute-done | bytes 294944 | tf_op jit(solution)/shard_map/ppermute | solution.py:185
  315.0 0.1 select_select_fusion.3
  315.1 1.7 divide_bitcast_fusion
  (12 shorter events, 0.0 us)
Async XLA Ops:
  4.1 48.9 %collective-permute-start.7 = (bf16[768,1536]{1,0:T(8,128)(2,1)S(1)}, bf16[768,1536]{1,0:T(8,128)(2,1)}, u32[]{:S(2)}, u32[]{:S(2)}) collective-permute-start(bf16[768,1536]{1,0:T(8,128)(2,1)S(1)} %get-tuple-element.64), channel_id=1, source_target_pairs={{0,2},{4,6},{9,11},{13,15},{18,16},{22,20},{27,25},{31,29}} | collective-permute-start | bytes 7077896 | tf_op jit(solution)/shard_map/ppermute | solution.py:185
  10.1 17.7 %collective-permute-start.2 = (bf16[176,1536]{1,0:T(8,128)(2,1)}, bf16[176,1536]{1,0:T(8,128)(2,1)}, u32[]{:S(2)}, u32[]{:S(2)}) collective-permute-start(bf16[176,1536]{1,0:T(8,128)(2,1)} %get-tuple-element.32), channel_id=1, source_target_pairs={{0,8},{4,12},{8,16},{12,20},{16,24},{20,28},{24,0},{28,4},{1,9},{5... | collective-permute-start | bytes 1622024 | tf_op jit(solution)/shard_map/ppermute | solution.py:185
  10.5 24.5 %collective-permute-start.1 = (bf16[176,1536]{1,0:T(8,128)(2,1)}, bf16[176,1536]{1,0:T(8,128)(2,1)}, u32[]{:S(2)}, u32[]{:S(2)}) collective-permute-start(bf16[176,1536]{1,0:T(8,128)(2,1)} %get-tuple-element.32), channel_id=1, source_target_pairs={{0,24},{4,28},{8,0},{12,4},{16,8},{20,12},{24,16},{28,20},{1,25},{... | collective-permute-start | bytes 1622024 | tf_op jit(solution)/shard_map/ppermute | solution.py:185
  12.7 22.3 %collective-permute-start = (bf16[176,1536]{1,0:T(8,128)(2,1)}, bf16[176,1536]{1,0:T(8,128)(2,1)}, u32[]{:S(2)}, u32[]{:S(2)}) collective-permute-start(bf16[176,1536]{1,0:T(8,128)(2,1)} %get-tuple-element.32), channel_id=1, source_target_pairs={{0,4},{4,0},{8,12},{12,8},{16,20},{20,16},{24,28},{28,24},{1,5},{5... | collective-permute-start | bytes 1622024 | tf_op jit(solution)/shard_map/ppermute | solution.py:185
  35.1 17.1 %collective-permute-start.5 = (bf16[176,1536]{1,0:T(8,128)(2,1)}, bf16[176,1536]{1,0:T(8,128)(2,1)S(1)}, u32[]{:S(2)}, u32[]{:S(2)}) collective-permute-start(bf16[176,1536]{1,0:T(8,128)(2,1)} %collective-permute-done.1.refs_4_), channel_id=1, source_target_pairs={{0,24},{4,28},{8,0},{12,4},{16,8},{20,12},{24,16},{28,20},{1,25},{... | collective-permute-start | bytes 1622024 | tf_op jit(solution)/shard_map/ppermute | solution.py:185
  37.2 37.1 %collective-permute-start.11 = (bf16[768,1536]{1,0:T(8,128)(2,1)}, bf16[768,1536]{1,0:T(8,128)(2,1)}, u32[]{:S(2)}, u32[]{:S(2)}) collective-permute-start(bf16[768,1536]{1,0:T(8,128)(2,1)} %get-tuple-element.63), channel_id=1, source_target_pairs={{0,2},{4,6},{9,11},{13,15},{18,16},{22,20},{27,25},{31,29}} | collective-permute-start | bytes 7077896 | tf_op jit(solution)/shard_map/ppermute | solution.py:185
  39.3 13.9 %collective-permute-start.8 = (bf16[176,1536]{1,0:T(8,128)(2,1)}, bf16[176,1536]{1,0:T(8,128)(2,1)}, u32[]{:S(2)}, u32[]{:S(2)}) collective-permute-start(bf16[176,1536]{1,0:T(8,128)(2,1)} %collective-permute-done.refs_2_), channel_id=1, source_target_pairs={{0,1},{1,0},{2,3},{3,2},{4,5},{5,4},{6,7},{7,6},{8,9},{9,8},{10,11... | collective-permute-start | bytes 1622024 | tf_op jit(solution)/shard_map/ppermute | solution.py:185
  52.1 22.2 %copy-start.3 = (bf16[176,1536]{1,0:T(8,128)(2,1)}, bf16[176,1536]{1,0:T(8,128)(2,1)S(1)}, u32[]{:S(2)}) copy-start(bf16[176,1536]{1,0:T(8,128)(2,1)S(1)} %collective-permute-done.5.refs_5_) | copy-start | bytes 1622020
  52.1 2.7 collective-permute-start.9
  52.9 2.7 collective-permute-start.10
  53.0 21.4 %collective-permute-start.4 = (bf16[176,1536]{1,0:T(8,128)(2,1)}, bf16[176,1536]{1,0:T(8,128)(2,1)S(1)}, u32[]{:S(2)}, u32[]{:S(2)}) collective-permute-start(bf16[176,1536]{1,0:T(8,128)(2,1)} %collective-permute-done.2.refs_6_), channel_id=1, source_target_pairs={{0,4},{4,0},{8,12},{12,8},{16,20},{20,16},{24,28},{28,24},{1,5},{5... | collective-permute-start | bytes 1622024 | tf_op jit(solution)/shard_map/ppermute | solution.py:185
  53.2 25.0 %collective-permute-start.3 = (bf16[176,1536]{1,0:T(8,128)(2,1)}, bf16[176,1536]{1,0:T(8,128)(2,1)}, u32[]{:S(2)}, u32[]{:S(2)}) collective-permute-start(bf16[176,1536]{1,0:T(8,128)(2,1)} %collective-permute-done.1.refs_4_), channel_id=1, source_target_pairs={{0,4},{4,0},{8,12},{12,8},{16,20},{20,16},{24,28},{28,24},{1,5},{5... | collective-permute-start | bytes 1622024 | tf_op jit(solution)/shard_map/ppermute | solution.py:185
  54.9 41.4 %collective-permute-start.14 = (bf16[176,1536]{1,0:T(8,128)(2,1)S(1)}, bf16[176,1536]{1,0:T(8,128)(2,1)}, u32[]{:S(2)}, u32[]{:S(2)}) collective-permute-start(bf16[176,1536]{1,0:T(8,128)(2,1)S(1)} %collective-permute-done.5.refs_5_), channel_id=1, source_target_pairs={{0,1},{1,0},{2,3},{3,2},{4,5},{5,4},{6,7},{7,6},{8,9},{9,8},{10,11... | collective-permute-start | bytes 1622024 | tf_op jit(solution)/shard_map/ppermute | solution.py:185
  55.6 34.1 %collective-permute-start.6 = (bf16[176,1536]{1,0:T(8,128)(2,1)S(1)}, bf16[176,1536]{1,0:T(8,128)(2,1)}, u32[]{:S(2)}, u32[]{:S(2)}) collective-permute-start(bf16[176,1536]{1,0:T(8,128)(2,1)S(1)} %collective-permute-done.5.refs_5_), channel_id=1, source_target_pairs={{0,4},{4,0},{8,12},{12,8},{16,20},{20,16},{24,28},{28,24},{1,5},{5... | collective-permute-start | bytes 1622024 | tf_op jit(solution)/shard_map/ppermute | solution.py:185
  74.3 20.6 %copy-start.4 = (bf16[176,1536]{1,0:T(8,128)(2,1)}, bf16[176,1536]{1,0:T(8,128)(2,1)S(1)}, u32[]{:S(2)}) copy-start(bf16[176,1536]{1,0:T(8,128)(2,1)S(1)} %collective-permute-done.4.refs_3_) | copy-start | bytes 1622020
  89.8 6.5 %collective-permute-start.12 = (bf16[176,1536]{1,0:T(8,128)(2,1)}, bf16[176,1536]{1,0:T(8,128)(2,1)}, u32[]{:S(2)}, u32[]{:S(2)}) collective-permute-start(bf16[176,1536]{1,0:T(8,128)(2,1)} %collective-permute-done.3.refs_1_), channel_id=1, source_target_pairs={{0,1},{1,0},{2,3},{3,2},{4,5},{5,4},{6,7},{7,6},{8,9},{9,8},{10,11... | collective-permute-start | bytes 1622024 | tf_op jit(solution)/shard_map/ppermute | solution.py:185
  91.1 5.2 %collective-permute-start.13 = (bf16[176,1536]{1,0:T(8,128)(2,1)S(1)}, bf16[176,1536]{1,0:T(8,128)(2,1)}, u32[]{:S(2)}, u32[]{:S(2)}) collective-permute-start(bf16[176,1536]{1,0:T(8,128)(2,1)S(1)} %collective-permute-done.4.refs_3_), channel_id=1, source_target_pairs={{0,1},{1,0},{2,3},{3,2},{4,5},{5,4},{6,7},{7,6},{8,9},{9,8},{10,11... | collective-permute-start | bytes 1622024 | tf_op jit(solution)/shard_map/ppermute | solution.py:185
  91.1 5.2 %collective-permute-start.15 = (bf16[176,1536]{1,0:T(8,128)(2,1)}, bf16[176,1536]{1,0:T(8,128)(2,1)}, u32[]{:S(2)}, u32[]{:S(2)}) collective-permute-start(bf16[176,1536]{1,0:T(8,128)(2,1)} %collective-permute-done.6.refs_7_), channel_id=1, source_target_pairs={{0,1},{1,0},{2,3},{3,2},{4,5},{5,4},{6,7},{7,6},{8,9},{9,8},{10,11... | collective-permute-start | bytes 1622024 | tf_op jit(solution)/shard_map/ppermute | solution.py:185
  95.0 21.3 %collective-permute-start.16 = (bf16[768,1536]{1,0:T(8,128)(2,1)}, bf16[768,1536]{1,0:T(8,128)(2,1)S(1)}, u32[]{:S(2)}, u32[]{:S(2)}) collective-permute-start(bf16[768,1536]{1,0:T(8,128)(2,1)} %broadcast_select_fusion), channel_id=1, source_target_pairs={{0,1},{2,3},{4,5},{6,7},{9,8},{11,10},{13,12},{15,14},{18,19},{16,... | collective-permute-start | bytes 7077896 | tf_op jit(solution)/shard_map/ppermute | solution.py:185
  125.9 1.9 copy-start.1
  125.9 60.4 %collective-permute-start.17 = (bf16[768,2560]{1,0:T(8,128)(2,1)S(1)}, bf16[768,2560]{1,0:T(8,128)(2,1)S(1)}, u32[]{:S(2)}, u32[]{:S(2)}) collective-permute-start(bf16[768,2560]{1,0:T(8,128)(2,1)S(1)} %convolution_convert_fusion.lrq_ref), channel_id=1, source_target_pairs={{0,1},{1,0},{2,3},{3,2},{4,5},{5,4},{6,7},{7,6},{8,9},{9,8},{10,11... | collective-permute-start | bytes 11796488 | tf_op jit(solution)/shard_map/ppermute | solution.py:185
  185.0 49.6 %collective-permute-start.18 = (bf16[1536,768]{1,0:T(8,128)(2,1)}, bf16[1536,768]{1,0:T(8,128)(2,1)}, u32[]{:S(2)}, u32[]{:S(2)}) collective-permute-start(bf16[1536,768]{1,0:T(8,128)(2,1)} %convolution_convert_fusion.1), channel_id=1, source_target_pairs={{0,1},{1,0},{2,3},{3,2},{4,5},{5,4},{6,7},{7,6},{8,9},{9,8},{10,11... | collective-permute-start | bytes 7077896 | tf_op jit(solution)/shard_map/ppermute | solution.py:185
  186.2 1.9 copy-start.2
  245.0 2.1 copy-start
  247.3 27.7 %collective-permute-start.19 = (bf16[4,192,768]{2,1,0:T(8,128)(2,1)S(1)}, bf16[4,192,768]{2,1,0:T(8,128)(2,1)S(1)}, u32[]{:S(2)}, u32[]{:S(2)}) collective-permute-start(bf16[4,192,768]{2,1,0:T(8,128)(2,1)S(1)} %fusion.5), channel_id=1, source_target_pairs={{0,2},{1,3},{2,0},{3,1},{4,6},{5,7},{6,4},{7,5},{8,10},{9,11},{10,... | collective-permute-start | bytes 3538952 | tf_op jit(solution)/shard_map/ppermute | solution.py:185
  277.0 25.0 %collective-permute-start.22 = (bf16[192,768]{1,0:T(8,128)(2,1)S(1)}, bf16[192,768]{1,0:T(8,128)(2,1)S(1)}, u32[]{:S(2)}, u32[]{:S(2)}) collective-permute-start(bf16[192,768]{1,0:T(8,128)(2,1)S(1)} %get-tuple-element.69), channel_id=1, source_target_pairs={{0,16},{1,24},{2,20},{3,28},{4,0},{5,8},{6,4},{7,12},{8,17},{9,25}... | collective-permute-start | bytes 884744 | tf_op jit(solution)/shard_map/ppermute | solution.py:185
  278.1 31.2 %collective-permute-start.23 = (bf16[192,768]{1,0:T(8,128)(2,1)S(1)}, bf16[192,768]{1,0:T(8,128)(2,1)S(1)}, u32[]{:S(2)}, u32[]{:S(2)}) collective-permute-start(bf16[192,768]{1,0:T(8,128)(2,1)S(1)} %get-tuple-element.70), channel_id=1, source_target_pairs={{0,24},{1,16},{2,28},{3,20},{4,8},{5,0},{6,12},{7,4},{8,25},{9,17}... | collective-permute-start | bytes 884744 | tf_op jit(solution)/shard_map/ppermute | solution.py:185
  282.1 27.2 %collective-permute-start.21 = (bf16[192,768]{1,0:T(8,128)(2,1)S(1)}, bf16[192,768]{1,0:T(8,128)(2,1)S(1)}, u32[]{:S(2)}, u32[]{:S(2)}) collective-permute-start(bf16[192,768]{1,0:T(8,128)(2,1)S(1)} %get-tuple-element.71), channel_id=1, source_target_pairs={{0,8},{1,0},{2,12},{3,4},{4,24},{5,16},{6,28},{7,20},{8,9},{9,1},{... | collective-permute-start | bytes 884744 | tf_op jit(solution)/shard_map/ppermute | solution.py:185
  282.1 32.9 %collective-permute-start.20 = (bf16[192,768]{1,0:T(8,128)(2,1)S(1)}, bf16[192,768]{1,0:T(8,128)(2,1)S(1)}, u32[]{:S(2)}, u32[]{:S(2)}) collective-permute-start(bf16[192,768]{1,0:T(8,128)(2,1)S(1)} %get-tuple-element.72), channel_id=1, source_target_pairs={{0,0},{1,8},{2,4},{3,12},{4,16},{5,24},{6,20},{7,28},{8,1},{9,9},{... | collective-permute-start | bytes 884744 | tf_op jit(solution)/shard_map/ppermute | solution.py:185
